TPU v7x, 128 devices: a whole 4x4x4 slice. The times are simulated.
128 devices in a mesh: gx: 16 (over x, z), gy: 8 (over y, core).
Axes of the slice: x: 4, y: 4, z: 4, core: 2. Of those that a mesh axis runs over, the one named last changes fastest.
Arguments:
- rhs_state: float32 [256, 512, 256], P('gx', 'gy'), may hold values from -100 to 100
- rhs_control: float32 [256, 512, 256], P('gx', 'gy'), may hold values from -100 to 100
- rhs_adjoint: float32 [256, 512, 256], P('gx', 'gy'), may hold values from -100 to 100
- barrier: float32 [256, 512, 256], P('gx', 'gy'), may hold values from 0.1 to 10
- active: int32 [256, 512, 256], P('gx', 'gy'), may hold values 0 or 1
Outputs:
- step_state: float32 [256, 512, 256], P('gx', 'gy')
- step_control: float32 [256, 512, 256], P('gx', 'gy')
- step_adjoint: float32 [256, 512, 256], P('gx', 'gy')
All inputs are finite; a program needn't handle non-finite values. No bound on the sum of `active` on one device may be relied on, other than what follows from the above.
Results may differ from a plain program's by a relative error of at most 0.0002.
Values sent between devices are 32-bit elements; how exact they have to be, the bound alone decides.
A program may use at most 64 MiB of HBM per device.

v0:
```python
import jax
import jax.numpy as jnp
from jax import lax
from jax.sharding import PartitionSpec as P

ITERS = 2
CHEB = 2


regular = 0.01
lower_edge = 0.5
upper_edge = 15.5


def padded_2(block, sides, width):
    for axis, dim in sides:
        count = lax.axis_size(axis)
        forward = [(i, i + 1) for i in range(count - 1)]
        forward.append((count - 1, 0))
        backward = [(target, source) for source, target in forward]
        low = lax.ppermute(
            lax.slice_in_dim(block, block.shape[dim] - width, None, axis=dim), axis, forward
        )
        high = lax.ppermute(lax.slice_in_dim(block, 0, width, axis=dim), axis, backward)
        block = jnp.concatenate([low, block, high], axis=dim)
    return block


def stencil(padded, damping):
    center = padded[..., 1:-1, 1:-1, :]
    neighbours = padded[..., 2:, 1:-1, :] + padded[..., :-2, 1:-1, :]
    zpadded = jnp.pad(center, [(0, 0)] * (center.ndim - 1) + [(1, 1)])
    neighbours = (
        neighbours
        + padded[..., 1:-1, 2:, :]
        + padded[..., 1:-1, :-2, :]
        + zpadded[..., 2:]
        + zpadded[..., :-2]
    )
    return (6.0 + damping) * center - neighbours


def local_inner(first, second):
    return (
        jnp.sum(first[0] * second[0])
        + jnp.sum(first[1] * second[1])
        + jnp.sum(first[2] * second[2])
    )


def energy_sum(first, second):
    return lax.psum(local_inner(first, second), ("gx", "gy"))


def cheb_numbers():
    centre = 0.5 * (upper_edge + lower_edge)
    half_span = 0.5 * (upper_edge - lower_edge)
    stretch = centre / half_span
    ratios = []
    ratio_old = 1.0 / stretch
    for counter in range(CHEB):
        ratio_now = 1.0 / (2.0 * stretch - ratio_old)
        ratios.append((ratio_now * ratio_old, 2.0 * ratio_now / half_span))
        ratio_old = ratio_now
    return (centre, ratios)


def chebyshev_single(rhs, damping, inside_rim):
    centre, ratios = cheb_numbers()
    approx = rhs / centre
    heading = approx
    for counter in range(CHEB):
        padded = padded_2(approx, (("gx", 0), ("gy", 1)), 1) * inside_rim
        residual = rhs - stencil(padded, damping)
        heading = ratios[counter][0] * heading + ratios[counter][1] * residual
        approx = approx + heading
    return approx


def rotation(
    delta_now,
    gamma_now,
    gamma_next,
    cos_old,
    cos_now,
    sin_old,
    sin_now,
    precond_now,
    search_old,
    search_now,
    iterate,
    eta_value,
):
    alpha_zero = cos_now * delta_now - cos_old * sin_now * gamma_now
    alpha_one = jnp.sqrt(alpha_zero * alpha_zero + gamma_next * gamma_next)
    alpha_two = sin_now * delta_now + cos_old * cos_now * gamma_now
    alpha_three = sin_old * gamma_now
    cos_new = alpha_zero / alpha_one
    sin_new = gamma_next / alpha_one
    search_new = tuple(
        (
            (p - alpha_three * a - alpha_two * b) / alpha_one
            for p, a, b in zip(precond_now, search_old, search_now)
        )
    )
    iterate = tuple((i + cos_new * eta_value * s for i, s in zip(iterate, search_new)))
    eta_value = -sin_new * eta_value
    return (cos_now, cos_new, sin_now, sin_new, search_now, search_new, iterate, eta_value)


def shards(rhs_state, rhs_control, rhs_adjoint, barrier, active):
    cells_x, cells_y, cells_z = rhs_state.shape
    position = lax.axis_index("gy")
    total_rows = cells_y * lax.axis_size("gy")

    def inside(rim_width):
        global_row = position * cells_y + jnp.arange(cells_y + 2 * rim_width) - rim_width
        return ((global_row >= 0) & (global_row < total_rows)).astype(jnp.float32).reshape(-1, 1)

    rim_masks = [inside(level) for level in range(2 * CHEB + 1)]
    inside_rim = rim_masks[1]
    fixed_mask = active.astype(jnp.float32)
    open_mask = 1.0 - fixed_mask
    control_diag = open_mask * (regular + barrier) + fixed_mask
    damping = open_mask / jnp.sqrt(regular + barrier)

    def solve_twice(rhs):
        first = chebyshev_single(rhs, damping, inside_rim)
        return chebyshev_single(first, damping, inside_rim)

    def precondition(vector):
        return (vector[0], vector[1] / control_diag, solve_twice(vector[2]))

    zeros = jnp.zeros_like(rhs_state)
    lanczos_old = (zeros, zeros, zeros)
    lanczos_now = (rhs_state, rhs_control, rhs_adjoint)
    gamma_old = jnp.float32(1.0)
    cos_old = jnp.float32(1.0)
    cos_now = jnp.float32(1.0)
    sin_old = jnp.float32(0.0)
    sin_now = jnp.float32(0.0)
    search_old = (zeros, zeros, zeros)
    search_now = (zeros, zeros, zeros)
    iterate = (zeros, zeros, zeros)
    precond = precondition(lanczos_now)
    gamma_now = jnp.sqrt(energy_sum(precond, lanczos_now))
    eta_value = gamma_now
    for iteration in range(ITERS):
        precond_now = tuple((f / gamma_now for f in precond))
        state_part, control, adjoint = precond_now
        stacked = jnp.stack([state_part, adjoint])
        padded = padded_2(stacked, (("gx", 1), ("gy", 2)), 1) * inside_rim
        images = stencil(padded, 0.0)
        image_now = (
            state_part + images[1],
            open_mask * ((regular + barrier) * control - adjoint) + fixed_mask * control,
            images[0] - open_mask * control,
        )
        delta_now = lax.psum(local_inner(image_now, precond_now), ("gx", "gy"))
        coef_one = delta_now / gamma_now
        coef_two = gamma_now / gamma_old
        lanczos_next = tuple(
            (
                a - coef_one * b - coef_two * c
                for a, b, c in zip(image_now, lanczos_now, lanczos_old)
            )
        )
        precond = precondition(lanczos_next)
        gamma_next = jnp.sqrt(energy_sum(precond, lanczos_next))
        cos_old, cos_now, sin_old, sin_now, search_old, search_now, iterate, eta_value = rotation(
            delta_now,
            gamma_now,
            gamma_next,
            cos_old,
            cos_now,
            sin_old,
            sin_now,
            precond_now,
            search_old,
            search_now,
            iterate,
            eta_value,
        )
        lanczos_old, lanczos_now = (lanczos_now, lanczos_next)
        gamma_old, gamma_now = (gamma_now, gamma_next)
    return (iterate[0], iterate[1], iterate[2])


def solution(mesh):
    placed = (
        P("gx", "gy", None),
        P("gx", "gy", None),
        P("gx", "gy", None),
        P("gx", "gy", None),
        P("gx", "gy", None),
    )
    return jax.shard_map(
        shards,
        mesh=mesh,
        in_specs=placed,
        out_specs=(P("gx", "gy", None), P("gx", "gy", None), P("gx", "gy", None)),
        check_vma=False,
    )
```

profile of v0, /device:TPU:1, one launch (start us, length us, event | category | flops | bytes accessed | tf_op | source)
XLA Modules:
  0.0 575.5 jit_solution(5273647928370668800)
XLA Ops:
  2.0 6.8 %collective-permute-start.1 = (f32[1,64,256]{2,1,0:T(8,128)S(1)}, f32[1,64,256]{2,1,0:T(8,128)S(1)}, u32[]{:S(2)}, u32[]{:S(2)}) collective-permute-start(f32[1,64,256]{2,1,0:T(8,128)S(1)} %get-tuple-element.100), channel_id=1, source_target_pairs={{8,0},{16,8},{24,16},{32,24},{40,32},{48,40},{56,48},{64,56},{72,6... | collective-permute-start | bytes 196616 | tf_op jit(solution)/shard_map/ppermute | solution.py:24
  10.1 5.1 collective-permute-done
  15.3 2.1 collective-permute-start.3
  27.1 3.4 collective-permute-done.4
  30.6 4.2 collective-permute-start.7
  40.5 3.4 collective-permute-done.8
  43.9 4.4 collective-permute-start.11
  49.9 1.9 fusion.94
  55.0 3.4 collective-permute-done.12
  58.4 4.4 collective-permute-start.15
  69.3 64.1 %psum.35 = f32[]{:T(128)} all-reduce(f32[]{:T(128)S(6)} %add.463), channel_id=1, replica_groups=mesh['gx'=16,'gy'=8] {'gx','gy'}, use_global_device_ids=true, to_apply=%region_3.4 | all-reduce | flops 1 | bytes 8 | tf_op jit(solution)/shard_map/psum | solution.py:52
  134.4 2.4 collective-permute-start.17
  139.1 5.4 collective-permute-done.16
  144.5 2.1 collective-permute-start.19
  154.3 64.7 %psum.36 = f32[]{:T(128)} all-reduce(f32[]{:T(128)S(6)} %add.472), channel_id=1, replica_groups=mesh['gx'=16,'gy'=8] {'gx','gy'}, use_global_device_ids=true, to_apply=%region_7.8 | all-reduce | flops 1 | bytes 8 | tf_op jit(solution)/shard_map/psum | solution.py:159
  219.7 5.6 broadcast_multiply_fusion.3
  225.3 2.4 collective-permute-start.21
  229.1 5.1 collective-permute-done.20
  234.2 2.1 collective-permute-start.23
  241.9 3.4 collective-permute-done.24
  245.4 4.4 collective-permute-start.27
  255.6 3.4 collective-permute-done.28
  259.0 4.4 collective-permute-start.31
  264.9 1.9 fusion.96
  270.2 3.4 collective-permute-done.32
  273.6 4.4 collective-permute-start.35
  282.5 2.7 multiply_reduce_fusion.4
  285.8 64.4 %psum.37 = f32[]{:T(128)} all-reduce(f32[]{:T(128)S(6)} %add.502), channel_id=1, replica_groups=mesh['gx'=16,'gy'=8] {'gx','gy'}, use_global_device_ids=true, to_apply=%region_11.12 | all-reduce | flops 1 | bytes 8 | tf_op jit(solution)/shard_map/psum | solution.py:52
  352.5 2.4 collective-permute-start.37
  355.0 2.2 collective-permute-done.37
  357.2 4.9 collective-permute-done.36
  362.2 2.1 collective-permute-start.39
  368.5 2.9 multiply_reduce_fusion.1
  373.4 64.7 %psum.38 = f32[]{:T(128)} all-reduce(f32[]{:T(128)S(6)} %add.513), channel_id=1, replica_groups=mesh['gx'=16,'gy'=8] {'gx','gy'}, use_global_device_ids=true, to_apply=%region_15.16 | all-reduce | flops 1 | bytes 8 | tf_op jit(solution)/shard_map/psum | solution.py:159
  438.7 2.1 broadcast_multiply_fusion.1
  440.9 2.4 collective-permute-start.41
  444.6 5.1 collective-permute-done.40
  449.8 2.1 collective-permute-start.43
  457.5 3.6 collective-permute-done.44
  461.2 4.4 collective-permute-start.47
  467.1 2.0 broadcast_multiply_fusion
  472.3 3.4 collective-permute-done.48
  475.7 4.4 collective-permute-start.51
  484.3 1.9 fusion.98
  489.6 3.2 collective-permute-done.52
  492.9 4.1 collective-permute-start.55
  505.8 64.1 %psum.39 = f32[]{:T(128)} all-reduce(f32[]{:T(128)S(6)} %add.543), channel_id=1, replica_groups=mesh['gx'=16,'gy'=8] {'gx','gy'}, use_global_device_ids=true, to_apply=%region_19.20 | all-reduce | flops 1 | bytes 8 | tf_op jit(solution)/shard_map/psum | solution.py:52
  570.7 4.6 multiply_add_fusion
  (233 shorter events, 85.5 us)
Async XLA Ops:
  2.0 8.2 %collective-permute-start.1 = (f32[1,64,256]{2,1,0:T(8,128)S(1)}, f32[1,64,256]{2,1,0:T(8,128)S(1)}, u32[]{:S(2)}, u32[]{:S(2)}) collective-permute-start(f32[1,64,256]{2,1,0:T(8,128)S(1)} %get-tuple-element.100), channel_id=1, source_target_pairs={{8,0},{16,8},{24,16},{32,24},{40,32},{48,40},{56,48},{64,56},{72,6... | collective-permute-start | bytes 196616 | tf_op jit(solution)/shard_map/ppermute | solution.py:24
  8.8 6.4 %collective-permute-start = (f32[1,64,256]{2,1,0:T(8,128)S(1)}, f32[1,64,256]{2,1,0:T(8,128)S(1)}, u32[]{:S(2)}, u32[]{:S(2)}) collective-permute-start(f32[1,64,256]{2,1,0:T(8,128)S(1)} %get-tuple-element.99), channel_id=1, source_target_pairs={{0,8},{8,16},{16,24},{24,32},{32,40},{40,48},{48,56},{56,64},{64,7... | collective-permute-start | bytes 196616 | tf_op jit(solution)/shard_map/ppermute | solution.py:21
  15.3 4.7 collective-permute-start.3
  17.4 2.6 collective-permute-start.2
  23.9 3.2 collective-permute-start.5
  24.0 6.5 %collective-permute-start.4 = (f32[1,64,256]{2,1,0:T(8,128)S(1)}, f32[1,64,256]{2,1,0:T(8,128)S(1)}, u32[]{:S(2)}, u32[]{:S(2)}) collective-permute-start(f32[1,64,256]{2,1,0:T(8,128)S(1)} %get-tuple-element.97), channel_id=1, source_target_pairs={{0,8},{8,16},{16,24},{24,32},{32,40},{40,48},{48,56},{56,64},{64,7... | collective-permute-start | bytes 196616 | tf_op jit(solution)/shard_map/ppermute | solution.py:21
  30.6 5.0 collective-permute-start.7
  37.3 3.2 collective-permute-start.9
  37.4 6.5 %collective-permute-start.8 = (f32[1,64,256]{2,1,0:T(8,128)S(1)}, f32[1,64,256]{2,1,0:T(8,128)S(1)}, u32[]{:S(2)}, u32[]{:S(2)}) collective-permute-start(f32[1,64,256]{2,1,0:T(8,128)S(1)} %get-tuple-element.95), channel_id=1, source_target_pairs={{0,8},{8,16},{16,24},{24,32},{32,40},{40,48},{48,56},{56,64},{64,7... | collective-permute-start | bytes 196616 | tf_op jit(solution)/shard_map/ppermute | solution.py:21
  43.9 5.2 collective-permute-start.11
  51.8 3.2 collective-permute-start.13
  51.9 6.5 %collective-permute-start.12 = (f32[1,64,256]{2,1,0:T(8,128)S(1)}, f32[1,64,256]{2,1,0:T(8,128)S(1)}, u32[]{:S(2)}, u32[]{:S(2)}) collective-permute-start(f32[1,64,256]{2,1,0:T(8,128)S(1)} %get-tuple-element.93), channel_id=1, source_target_pairs={{0,8},{8,16},{16,24},{24,32},{32,40},{40,48},{48,56},{56,64},{64,7... | collective-permute-start | bytes 196616 | tf_op jit(solution)/shard_map/ppermute | solution.py:21
  58.4 6.6 %collective-permute-start.15 = (f32[18,1,256]{2,1,0:T(1,128)S(1)}, f32[18,1,256]{2,1,0:T(1,128)S(1)}, u32[]{:S(2)}, u32[]{:S(2)}) collective-permute-start(f32[18,1,256]{2,1,0:T(1,128)S(1)} %get-tuple-element.68), channel_id=1, source_target_pairs={{1,0},{2,1},{3,2},{4,3},{5,4},{6,5},{7,6},{0,7},{9,8},{10,9},{11,1... | collective-permute-start | bytes 55304 | tf_op jit(solution)/shard_map/ppermute | solution.py:24
  62.8 2.3 collective-permute-start.14
  134.4 4.6 collective-permute-start.17
  136.9 7.6 %collective-permute-start.16 = (f32[2,1,64,256]{3,2,1,0:T(8,128)S(1)}, f32[2,1,64,256]{3,2,1,0:T(8,128)S(1)}, u32[]{:S(2)}, u32[]{:S(2)}) collective-permute-start(f32[2,1,64,256]{3,2,1,0:T(8,128)S(1)} %get-tuple-element.48), channel_id=1, source_target_pairs={{0,8},{8,16},{16,24},{24,32},{32,40},{40,48},{48,56},{56,64},{64,7... | collective-permute-start | bytes 393224 | tf_op jit(solution)/shard_map/ppermute | solution.py:21
  144.5 3.4 collective-permute-start.19
  146.6 1.3 collective-permute-start.18
  225.3 3.8 collective-permute-start.21
  227.7 6.4 %collective-permute-start.20 = (f32[1,64,256]{2,1,0:T(8,128)S(1)}, f32[1,64,256]{2,1,0:T(8,128)S(1)}, u32[]{:S(2)}, u32[]{:S(2)}) collective-permute-start(f32[1,64,256]{2,1,0:T(8,128)S(1)} %get-tuple-element.91), channel_id=1, source_target_pairs={{0,8},{8,16},{16,24},{24,32},{32,40},{40,48},{48,56},{56,64},{64,7... | collective-permute-start | bytes 196616 | tf_op jit(solution)/shard_map/ppermute | solution.py:21
  234.2 3.2 collective-permute-start.23
  238.8 3.2 collective-permute-start.25
  238.8 6.5 %collective-permute-start.24 = (f32[1,64,256]{2,1,0:T(8,128)S(1)}, f32[1,64,256]{2,1,0:T(8,128)S(1)}, u32[]{:S(2)}, u32[]{:S(2)}) collective-permute-start(f32[1,64,256]{2,1,0:T(8,128)S(1)} %get-tuple-element.89), channel_id=1, source_target_pairs={{0,8},{8,16},{16,24},{24,32},{32,40},{40,48},{48,56},{56,64},{64,7... | collective-permute-start | bytes 196616 | tf_op jit(solution)/shard_map/ppermute | solution.py:21
  245.4 5.2 collective-permute-start.27
  252.4 3.2 collective-permute-start.29
  252.5 6.5 %collective-permute-start.28 = (f32[1,64,256]{2,1,0:T(8,128)S(1)}, f32[1,64,256]{2,1,0:T(8,128)S(1)}, u32[]{:S(2)}, u32[]{:S(2)}) collective-permute-start(f32[1,64,256]{2,1,0:T(8,128)S(1)} %get-tuple-element.87), channel_id=1, source_target_pairs={{0,8},{8,16},{16,24},{24,32},{32,40},{40,48},{48,56},{56,64},{64,7... | collective-permute-start | bytes 196616 | tf_op jit(solution)/shard_map/ppermute | solution.py:21
  259.0 5.2 collective-permute-start.31
  266.8 3.4 collective-permute-start.33
  267.1 6.5 %collective-permute-start.32 = (f32[1,64,256]{2,1,0:T(8,128)S(1)}, f32[1,64,256]{2,1,0:T(8,128)S(1)}, u32[]{:S(2)}, u32[]{:S(2)}) collective-permute-start(f32[1,64,256]{2,1,0:T(8,128)S(1)} %get-tuple-element.85), channel_id=1, source_target_pairs={{0,8},{8,16},{16,24},{24,32},{32,40},{40,48},{48,56},{56,64},{64,7... | collective-permute-start | bytes 196616 | tf_op jit(solution)/shard_map/ppermute | solution.py:21
  273.6 5.8 %collective-permute-start.35 = (f32[18,1,256]{2,1,0:T(1,128)S(1)}, f32[18,1,256]{2,1,0:T(1,128)S(1)}, u32[]{:S(2)}, u32[]{:S(2)}) collective-permute-start(f32[18,1,256]{2,1,0:T(1,128)S(1)} %get-tuple-element.60), channel_id=1, source_target_pairs={{1,0},{2,1},{3,2},{4,3},{5,4},{6,5},{7,6},{0,7},{9,8},{10,9},{11,1... | collective-permute-start | bytes 55304 | tf_op jit(solution)/shard_map/ppermute | solution.py:24
  278.0 1.4 collective-permute-start.34
  352.5 4.6 collective-permute-start.37
  355.0 7.1 %collective-permute-start.36 = (f32[2,1,64,256]{3,2,1,0:T(8,128)S(1)}, f32[2,1,64,256]{3,2,1,0:T(8,128)S(1)}, u32[]{:S(2)}, u32[]{:S(2)}) collective-permute-start(f32[2,1,64,256]{3,2,1,0:T(8,128)S(1)} %get-tuple-element.44), channel_id=1, source_target_pairs={{0,8},{8,16},{16,24},{24,32},{32,40},{40,48},{48,56},{56,64},{64,7... | collective-permute-start | bytes 393224 | tf_op jit(solution)/shard_map/ppermute | solution.py:21
  362.2 3.4 collective-permute-start.39
  440.9 3.8 collective-permute-start.41
  443.3 6.4 %collective-permute-start.40 = (f32[1,64,256]{2,1,0:T(8,128)S(1)}, f32[1,64,256]{2,1,0:T(8,128)S(1)}, u32[]{:S(2)}, u32[]{:S(2)}) collective-permute-start(f32[1,64,256]{2,1,0:T(8,128)S(1)} %get-tuple-element.83), channel_id=1, source_target_pairs={{0,8},{8,16},{16,24},{24,32},{32,40},{40,48},{48,56},{56,64},{64,7... | collective-permute-start | bytes 196616 | tf_op jit(solution)/shard_map/ppermute | solution.py:21
  449.8 3.2 collective-permute-start.43
  454.3 3.2 collective-permute-start.45
  454.4 6.7 %collective-permute-start.44 = (f32[1,64,256]{2,1,0:T(8,128)S(1)}, f32[1,64,256]{2,1,0:T(8,128)S(1)}, u32[]{:S(2)}, u32[]{:S(2)}) collective-permute-start(f32[1,64,256]{2,1,0:T(8,128)S(1)} %get-tuple-element.81), channel_id=1, source_target_pairs={{0,8},{8,16},{16,24},{24,32},{32,40},{40,48},{48,56},{56,64},{64,7... | collective-permute-start | bytes 196616 | tf_op jit(solution)/shard_map/ppermute | solution.py:21
  461.2 5.2 collective-permute-start.47
  469.1 3.2 collective-permute-start.49
  469.2 6.5 %collective-permute-start.48 = (f32[1,64,256]{2,1,0:T(8,128)S(1)}, f32[1,64,256]{2,1,0:T(8,128)S(1)}, u32[]{:S(2)}, u32[]{:S(2)}) collective-permute-start(f32[1,64,256]{2,1,0:T(8,128)S(1)} %get-tuple-element.79), channel_id=1, source_target_pairs={{0,8},{8,16},{16,24},{24,32},{32,40},{40,48},{48,56},{56,64},{64,7... | collective-permute-start | bytes 196616 | tf_op jit(solution)/shard_map/ppermute | solution.py:21
  475.7 5.9 %collective-permute-start.51 = (f32[18,1,256]{2,1,0:T(1,128)S(1)}, f32[18,1,256]{2,1,0:T(1,128)S(1)}, u32[]{:S(2)}, u32[]{:S(2)}) collective-permute-start(f32[18,1,256]{2,1,0:T(1,128)S(1)} %get-tuple-element.54), channel_id=1, source_target_pairs={{1,0},{2,1},{3,2},{4,3},{5,4},{6,5},{7,6},{0,7},{9,8},{10,9},{11,1... | collective-permute-start | bytes 55304 | tf_op jit(solution)/shard_map/ppermute | solution.py:24
  480.1 1.5 collective-permute-start.50
  486.2 3.3 collective-permute-start.53
  486.3 6.5 %collective-permute-start.52 = (f32[1,64,256]{2,1,0:T(8,128)S(1)}, f32[1,64,256]{2,1,0:T(8,128)S(1)}, u32[]{:S(2)}, u32[]{:S(2)}) collective-permute-start(f32[1,64,256]{2,1,0:T(8,128)S(1)} %get-tuple-element.77), channel_id=1, source_target_pairs={{0,8},{8,16},{16,24},{24,32},{32,40},{40,48},{48,56},{56,64},{64,7... | collective-permute-start | bytes 196616 | tf_op jit(solution)/shard_map/ppermute | solution.py:21
  492.9 7.5 %collective-permute-start.55 = (f32[18,1,256]{2,1,0:T(1,128)S(1)}, f32[18,1,256]{2,1,0:T(1,128)S(1)}, u32[]{:S(2)}, u32[]{:S(2)}) collective-permute-start(f32[18,1,256]{2,1,0:T(1,128)S(1)} %get-tuple-element.52), channel_id=1, source_target_pairs={{1,0},{2,1},{3,2},{4,3},{5,4},{6,5},{7,6},{0,7},{9,8},{10,9},{11,1... | collective-permute-start | bytes 55304 | tf_op jit(solution)/shard_map/ppermute | solution.py:24
  496.9 3.4 collective-permute-start.54
  (48 other events, 200.2 us)
where the time goes:
time: 585 us; the launch traced here: 575 us
  blocking collectives  322 us (55%)
  waiting for transfers between devices  89.5 us (15%)
  starting transfers between devices  81.9 us (14%)
  other arithmetic  53 us (9%)
  between operations  17.8 us (3%)
  local copies, waits for them, and re-layouts  11.2 us (2%)
    psum x3, blocking collectives, energy_sum(): return lax.psum(local_inner(first, second), ('gx', 'gy'))  193 us
    psum x2, blocking collectives, shards(): delta_now = lax.psum(local_inner(image_now, precond_now), ('gx', 'gy'))  129 us
    ppermute x28, starting transfers between devices, padded_2(): lax.ppermute(lax.slice_in_dim(block, 0, width, axis=dim), axis, backward)  67 us
    ppermute x28, waiting for transfers between devices, padded_2(): lax.ppermute(lax.slice_in_dim(block, block.shape[dim] - width, None, axis...  58.2 us
    ppermute x28, waiting for transfers between devices, padded_2(): lax.ppermute(lax.slice_in_dim(block, 0, width, axis=dim), axis, backward)  31.3 us
    ppermute x28, starting transfers between devices, padded_2(): lax.ppermute(lax.slice_in_dim(block, block.shape[dim] - width, None, axis...  15 us
    div x6, other arithmetic, chebyshev_single(): approx = rhs / centre  13.1 us
  transfers between devices with their start and end apart: 56, of which 44 were waited for; matrix products, arithmetic and copies ran while one was open for 1% of the time, Pallas kernels for 0%

commit v1 on v0

v1 whole, which is shorter than its diff:
```python
import functools

import jax
import jax.numpy as jnp
from jax import lax
from jax.experimental import pallas as pl
from jax.experimental.pallas import tpu as pltpu
from jax.sharding import PartitionSpec as P

REGULAR = 0.01
CENTRE = 8.0
HALF = 7.5
STRETCH = CENTRE / HALF
Q0 = 1.0 / STRETCH
Q1 = 1.0 / (2.0 * STRETCH - Q0)
Q2 = 1.0 / (2.0 * STRETCH - Q1)
A1, B1 = Q1 * Q0, 2.0 * Q1 / HALF
A2, B2 = Q2 * Q1, 2.0 * Q2 / HALF
K1 = 1.0 + A1 + B1 * (CENTRE - 6.0)
K2 = 1.0 + A2 - 6.0 * B2
KR = B2 * CENTRE - A2
INV = 1.0 / CENTRE
INV2 = INV * INV

C1, V1A, Y1, QC, U1, YQ, Y1B, UQ, P1, YQB, QA, P2, RC, YR = range(14)
FIELDS = 14
LANES = 128
SUB = 8
RIGHT, LEFT, UP, DOWN = range(4)
MESH = pl.DeviceIdType.MESH


def kernel(
    nx,
    ny,
    nz,
    va_in,
    vb_in,
    vc_in,
    bar_in,
    act_in,
    out_a,
    out_b,
    out_c,
    raw,
    raw_act,
    fld,
    aux,
    res,
    ysend,
    yhalo,
    ar1,
    ar2,
    in_sem,
    out_sem,
    send_sem,
    recv_sem,
    ar_send,
    ar_recv,
):
    gx, gy = lax.axis_index("gx"), lax.axis_index("gy")
    mx, my = lax.axis_size("gx"), lax.axis_size("gy")
    nt = ny // SUB
    halves = nz // LANES
    right, left = lax.rem(gx + 1, mx), lax.rem(gx + mx - 1, mx)

    inputs = ((vc_in, raw.at[0]), (va_in, raw.at[1]), (act_in, raw_act), (bar_in, raw.at[2]), (vb_in, raw.at[3]))
    loads = [
        [
            pltpu.make_async_copy(src.at[:, :, pl.ds(h * LANES, LANES)], dst.at[h], in_sem.at[i, h])
            for h in range(halves)
        ]
        for i, (src, dst) in enumerate(inputs)
    ]
    for load in loads:
        for part in load:
            part.start()

    def wait_load(i):
        for part in loads[i]:
            part.wait()

    barrier = pltpu.get_barrier_semaphore()

    def greet_gy(k, carry):
        pl.semaphore_signal(barrier, inc=1, device_id=(gx, lax.rem(gy + k, my)), device_id_type=MESH)
        return carry

    def greet_gx(k, carry):
        pl.semaphore_signal(barrier, inc=1, device_id=(lax.rem(gx + k, mx), gy), device_id_type=MESH)
        return carry

    lax.fori_loop(1, my, greet_gy, 0)
    lax.fori_loop(1, mx, greet_gx, 0)

    @pl.when(gy == 0)
    def _():
        for f in range(FIELDS):
            yhalo[f, 0] = jnp.zeros((nx, 1, nz), jnp.float32)

    @pl.when(gy == my - 1)
    def _():
        for f in range(FIELDS):
            yhalo[f, 1] = jnp.zeros((nx, 1, nz), jnp.float32)

    lane = lax.broadcasted_iota(jnp.int32, (SUB, LANES), 1)
    sub = lax.broadcasted_iota(jnp.int32, (SUB, LANES), 0)
    first_lane, last_lane = lane == 0, lane == LANES - 1
    first_sub, last_sub = sub == 0, sub == SUB - 1
    zero = jnp.zeros((SUB, LANES), jnp.float32)

    def span(h):
        return pl.ds(h * LANES, LANES)

    def copy_to(f, way):
        if way == RIGHT:
            src, dst, device = fld.at[f, nx], fld.at[f, 0], (right, gy)
        elif way == LEFT:
            src, dst, device = fld.at[f, 1], fld.at[f, nx + 1], (left, gy)
        elif way == UP:
            src, dst, device = ysend.at[f, 1], yhalo.at[f, 0], (gx, gy + 1)
        else:
            src, dst, device = ysend.at[f, 0], yhalo.at[f, 1], (gx, gy - 1)
        return pltpu.make_async_remote_copy(
            src_ref=src,
            dst_ref=dst,
            send_sem=send_sem.at[f, way],
            recv_sem=recv_sem.at[f, way],
            device_id=device,
            device_id_type=MESH,
        )

    def send_x(f):
        copy_to(f, RIGHT).start()
        copy_to(f, LEFT).start()

    def send_y(f):
        @pl.when(gy < my - 1)
        def _():
            copy_to(f, UP).start()

        @pl.when(gy > 0)
        def _():
            copy_to(f, DOWN).start()

    def wait_halo(f):
        copy_to(f, RIGHT).wait_recv()
        copy_to(f, LEFT).wait_recv()

        @pl.when(gy > 0)
        def _():
            copy_to(f, UP).wait_recv()

        @pl.when(gy < my - 1)
        def _():
            copy_to(f, DOWN).wait_recv()

    def wait_sent(f):
        copy_to(f, RIGHT).wait_send()
        copy_to(f, LEFT).wait_send()

        @pl.when(gy < my - 1)
        def _():
            copy_to(f, UP).wait_send()

        @pl.when(gy > 0)
        def _():
            copy_to(f, DOWN).wait_send()

    def put(f, x, t, h, value):
        fld[f, x + 1, t, :, span(h)] = value
        if t == 0:
            ysend[f, 0, x, :, span(h)] = value[0:1]
        if t == nt - 1:
            ysend[f, 1, x, :, span(h)] = value[SUB - 1 : SUB]

    def plane_sums(f, x):
        centre = [[fld[f, x + 1, t, :, span(h)] for h in range(halves)] for t in range(nt)]
        low = [yhalo[f, 0, x, :, span(h)] for h in range(halves)]
        high = [yhalo[f, 1, x, :, span(h)] for h in range(halves)]
        for t in range(nt):
            up = [pltpu.roll(v, 1, 1) for v in centre[t]]
            down = [pltpu.roll(v, LANES - 1, 1) for v in centre[t]]
            for h in range(halves):
                if t > 0:
                    before = centre[t - 1][h]
                else:
                    before = jnp.where(first_sub, low[h], pltpu.roll(centre[nt - 1][h], 1, 0))
                if t < nt - 1:
                    after = centre[t + 1][h]
                else:
                    after = jnp.where(last_sub, high[h], pltpu.roll(centre[0][h], SUB - 1, 0))
                below = jnp.where(first_lane, up[h - 1] if h > 0 else zero, up[h])
                above = jnp.where(last_lane, down[h + 1] if h < halves - 1 else zero, down[h])
                sides = fld[f, x, t, :, span(h)] + fld[f, x + 2, t, :, span(h)]
                yield t, h, centre[t][h], sides + (before + after) + (below + above)

    def stage(f_in, f_out, make, accs=()):
        def plane(x, accs):
            for t, h, v, total in plane_sums(f_in, x):
                value, terms = make(x, t, h, v, total)
                if f_out is not None:
                    put(f_out, x, t, h, value)
                accs = tuple(a + b for a, b in zip(accs, terms))
            return accs

        wait_halo(f_in)
        accs = lax.fori_loop(0, 2, lambda k, a: plane(k * (nx - 1), a), accs)
        if f_out is not None:
            send_x(f_out)
        accs = lax.fori_loop(1, nx - 1, plane, accs)
        if f_out is not None:
            send_y(f_out)
        return accs

    E1, E2, OPEN, ICD, VB = range(5)

    def at(f, x, t, h):
        return fld[f, x + 1, t, :, span(h)]

    def also(i, x, t, h):
        return aux[i, x, t, :, span(h)]

    def first_half(x, t, h, v, total):
        return also(E1, x, t, h) * v + B1 * total, ()

    def second_half(f_rhs):
        def make(x, t, h, v, total):
            return also(E2, x, t, h) * v + KR * at(f_rhs, x, t, h) + B2 * total, ()

        return make

    def strided(ref, x, t, h):
        return ref[h, x, pl.ds(t, SUB, stride=nt), :]

    def convert(i, f):
        def plane(x, carry):
            for t in range(nt):
                for h in range(halves):
                    put(f, x, t, h, strided(raw.at[i], x, t, h))
            return carry

        lax.fori_loop(0, nx, plane, 0)

    wait_load(0)
    convert(0, C1)
    wait_load(1)
    convert(1, V1A)
    pl.semaphore_wait(barrier, mx + my - 2)
    for f in (C1, V1A):
        send_x(f)
        send_y(f)
    for i in (2, 3, 4):
        wait_load(i)

    def prepare(x, acc):
        for t in range(nt):
            for h in range(halves):
                fixed = strided(raw_act, x, t, h).astype(jnp.float32)
                opened = 1.0 - fixed
                root = lax.rsqrt(REGULAR + strided(raw.at[2], x, t, h))
                damping = opened * root
                icd = damping * root + fixed
                vb = strided(raw.at[3], x, t, h)
                va = at(V1A, x, t, h)
                aux[E1, x, t, :, span(h)] = K1 - B1 * damping
                aux[E2, x, t, :, span(h)] = K2 - B2 * damping
                aux[OPEN, x, t, :, span(h)] = opened
                aux[ICD, x, t, :, span(h)] = icd
                aux[VB, x, t, :, span(h)] = vb
                acc = acc + (va * va + vb * vb * icd)
        return acc

    sum_ab = lax.fori_loop(0, nx, prepare, zero)

    def ar_copy(buf, i, phase, me, device):
        return pltpu.make_async_remote_copy(
            src_ref=buf.at[i, me],
            dst_ref=buf.at[i, me],
            send_sem=ar_send.at[i, phase],
            recv_sem=ar_recv.at[i, phase],
            device_id=device,
            device_id_type=MESH,
        )

    def ar_rows(i, rows):
        full = zero
        for k, row in enumerate(rows):
            full = jnp.where(sub == k, jnp.sum(row, axis=0, keepdims=True), full)
        ar1[i, gy] = full

        def go(k, carry):
            ar_copy(ar1, i, 0, gy, (gx, lax.rem(gy + k, my))).start()
            return carry

        lax.fori_loop(1, my, go, 0)

    def ar_wait(buf, i, phase, count, sem):
        whole = buf.at[i, pl.ds(0, count - 1)]
        pltpu.make_async_copy(whole, whole, sem.at[i, phase]).wait()

    def ar_middle(i):
        ar_wait(ar1, i, 0, my, ar_recv)
        full = ar1[i, 0]
        for k in range(1, my):
            full = full + ar1[i, k]
        ar2[i, gx] = full

        def go(k, carry):
            ar_copy(ar2, i, 1, gx, (lax.rem(gx + k, mx), gy)).start()
            return carry

        lax.fori_loop(1, mx, go, 0)

    def ar_end(i, count):
        ar_wait(ar2, i, 1, mx, ar_recv)
        full = ar2[i, 0]
        for k in range(1, mx):
            full = full + ar2[i, k]
        full = jnp.sum(full, axis=1, keepdims=True)
        return [jnp.broadcast_to(full[k : k + 1], (SUB, LANES)) for k in range(count)]

    def ar_sent(i):
        ar_wait(ar1, i, 0, my, ar_send)
        ar_wait(ar2, i, 1, mx, ar_send)

    def state_image(x, t, h, v, total):
        pb = also(VB, x, t, h) * also(ICD, x, t, h)
        return 6.0 * v - total - also(OPEN, x, t, h) * pb, ()

    def square_out(make):
        def made(x, t, h, v, total):
            value, _ = make(x, t, h, v, total)
            return value, (value * value,)

        return made

    stage(C1, Y1, first_half)
    stage(V1A, QC, state_image)
    (sum_u,) = stage(Y1, U1, square_out(second_half(C1)), (zero,))
    stage(QC, YQ, first_half)
    stage(U1, Y1B, first_half)
    stage(YQ, UQ, second_half(QC))

    def last_half(x, t, h, v, total):
        value, _ = second_half(U1)(x, t, h, v, total)
        return value, (value * at(QC, x, t, h),)

    (sum_qp,) = stage(Y1B, P1, last_half, (zero,))
    ar_rows(0, [sum_ab + INV2 * sum_u, sum_ab + (2.0 * INV2) * sum_qp])
    stage(UQ, YQB, first_half)
    ar_middle(0)

    def add_image(x, t, h, v, total):
        return at(V1A, x, t, h) + INV2 * (6.0 * v - total), ()

    stage(P1, QA, add_image)
    stage(YQB, P2, second_half(UQ))
    m0, m1 = ar_end(0, 2)
    shift = m1 / m0

    def adjoint_image(x, t, h, v, total):
        icd = also(ICD, x, t, h)
        part = also(OPEN, x, t, h) * icd * (also(VB, x, t, h) - INV2 * at(P1, x, t, h))
        return 6.0 * v - total - part - shift * at(QC, x, t, h), ()

    stage(QA, RC, adjoint_image)

    ZA, ZB, ZC = range(3)

    def close(x, t, h, v, total):
        va, qa, p1 = at(V1A, x, t, h), at(QA, x, t, h), at(P1, x, t, h)
        icd, opened, vb = also(ICD, x, t, h), also(OPEN, x, t, h), also(VB, x, t, h)
        za = qa - shift * va
        ra = za + INV2 * (6.0 * v - total) - shift * (qa - va)
        v2b = (1.0 - shift) * vb - opened * (INV2 * p1)
        zb = v2b * icd
        zc = INV2 * (v - shift * p1)
        rb = v2b - opened * zc
        u2 = at(UQ, x, t, h) - shift * at(U1, x, t, h)
        res[ZA, x, t, :, span(h)] = za
        res[ZB, x, t, :, span(h)] = zb
        res[ZC, x, t, :, span(h)] = zc
        base = za * za + zb * v2b
        return None, (
            base + INV2 * (u2 * u2),
            base + 2.0 * (at(RC, x, t, h) * zc),
            ra * ra + rb * rb * icd,
        )

    sums = stage(P2, None, close, (zero, zero, zero))
    stage(RC, YR, first_half)

    (sum_r,) = stage(YR, None, square_out(second_half(RC)), (zero,))
    ar_rows(1, [sums[0], sums[1], sums[2] + INV2 * sum_r])
    ar_middle(1)
    n2, top, m4 = ar_end(1, 3)

    d2 = top / n2
    g2sq = n2 / m0
    g2 = jnp.sqrt(g2sq)
    g3sq = jnp.maximum(m4 / n2 - d2 * d2 - g2sq, 0.0)
    a1 = jnp.sqrt(shift * shift + g2sq)
    c2, s2 = shift / a1, g2 / a1
    b0 = c2 * d2 - s2 * g2
    b1 = jnp.sqrt(b0 * b0 + g3sq)
    b2 = s2 * d2 + c2 * g2
    c3 = b0 / b1
    on_p = (c2 + c3 * s2 * b2 / b1) / a1
    on_z = -c3 / (b1 * a1)

    def finish(x, carry):
        for t in range(nt):
            for h in range(halves):
                where = (h, x, pl.ds(t, SUB, stride=nt))
                pb = also(VB, x, t, h) * also(ICD, x, t, h)
                raw[(0,) + where] = on_p * at(V1A, x, t, h) + on_z * res[ZA, x, t, :, span(h)]
                raw[(1,) + where] = on_p * pb + on_z * res[ZB, x, t, :, span(h)]
                raw[(2,) + where] = (INV2 * on_p) * at(P1, x, t, h) + on_z * res[ZC, x, t, :, span(h)]
        return carry

    parts = 4
    size = nx // parts
    stores = []
    for p in range(parts):
        lax.fori_loop(p * size, (p + 1) * size, finish, 0)
        for i, out in enumerate((out_a, out_b, out_c)):
            rows = pl.ds(p * size, size)
            for h in range(halves):
                store = pltpu.make_async_copy(
                    raw.at[i, h, rows], out.at[rows, :, pl.ds(h * LANES, LANES)], out_sem.at[i, p, h]
                )
                store.start()
                stores.append(store)
    for f in range(FIELDS):
        wait_sent(f)
    ar_sent(0)
    ar_sent(1)
    for store in stores:
        store.wait()


def shards(va, vb, vc, barrier, active):
    nx, ny, nz = va.shape
    mx, my = lax.axis_size("gx"), lax.axis_size("gy")
    f32 = jnp.float32
    nt = ny // SUB
    hbm = pl.BlockSpec(memory_space=pl.ANY)
    out = jax.ShapeDtypeStruct(va.shape, f32)
    return pl.pallas_call(
        functools.partial(kernel, nx, ny, nz),
        out_shape=(out, out, out),
        in_specs=[hbm] * 5,
        out_specs=(hbm, hbm, hbm),
        scratch_shapes=[
            pltpu.VMEM((4, nz // LANES, nx, ny, LANES), f32),
            pltpu.VMEM((nz // LANES, nx, ny, LANES), jnp.int32),
            pltpu.VMEM((FIELDS, nx + 2, nt, SUB, nz), f32),
            pltpu.VMEM((5, nx, nt, SUB, nz), f32),
            pltpu.VMEM((3, nx, nt, SUB, nz), f32),
            pltpu.VMEM((FIELDS, 2, nx, 1, nz), f32),
            pltpu.VMEM((FIELDS, 2, nx, 1, nz), f32),
            pltpu.VMEM((2, my, SUB, LANES), f32),
            pltpu.VMEM((2, mx, SUB, LANES), f32),
            pltpu.SemaphoreType.DMA((5, nz // LANES)),
            pltpu.SemaphoreType.DMA((3, 4, nz // LANES)),
            pltpu.SemaphoreType.DMA((FIELDS, 4)),
            pltpu.SemaphoreType.DMA((FIELDS, 4)),
            pltpu.SemaphoreType.DMA((2, 2)),
            pltpu.SemaphoreType.DMA((2, 2)),
        ],
        compiler_params=pltpu.CompilerParams(
            collective_id=0, has_side_effects=True, vmem_limit_bytes=48 * 1024 * 1024
        ),
    )(va, vb, vc, barrier, active)


def solution(mesh):
    placed = P("gx", "gy", None)
    return jax.shard_map(
        shards,
        mesh=mesh,
        in_specs=(placed,) * 5,
        out_specs=(placed,) * 3,
        check_vma=False,
    )
```

time: 585 us -> 69.3 us (0.12); the launches traced: 575 us -> 69.1 us
  blocking collectives: 322 us -> 0 us
  waiting for transfers between devices: 89.5 us -> 0 us
  starting transfers between devices: 81.9 us -> 0 us
  Pallas kernels: 0 us -> 63.1 us
  other arithmetic: 53 us -> 0 us
  between operations: 17.8 us -> 0.65 us
    psum x5 -> x0, blocking collectives: 322 us -> none  [the longest x3 193 us: energy_sum(): return lax.psum(local_inner(first, second), ('gx', 'gy'))]
    ppermute x56 -> x0, waiting for transfers between devices: 89.5 us -> none  [the longest x28 58.2 us: padded_2(): lax.ppermute(lax.slice_in_dim(block, block.shape[dim] - width, None, axis...]
    ppermute x56 -> x0, starting transfers between devices: 81.9 us -> none  [the longest x28 67 us: padded_2(): lax.ppermute(lax.slice_in_dim(block, 0, width, axis=dim), axis, backward)]
    pallas_call x0 -> x1, Pallas kernels: none -> 63.1 us  [shards(): pl.pallas_call(functools.partial(kernel, nx, ny, nz), out_shape=(out, out...]
    reduce_sum x8 -> x0, other arithmetic: 14.5 us -> none  [the longest x5 10.8 us: local_inner(): jnp.sum(first[2] * second[2])]
    add x7 -> x0, other arithmetic: 13.8 us -> none  [the longest x6 9.23 us: chebyshev_single(): approx = approx + heading]
    div x6 -> x0, other arithmetic: 13.1 us -> none  [chebyshev_single(): approx = rhs / centre]
    mul x14 -> x0, other arithmetic: 7.05 us -> none  [the longest x12 6.24 us: chebyshev_single(): padded = padded_2(approx, (('gx', 0), ('gy', 1)), 1) * inside_rim]
  transfers between devices with their start and end apart: 56 -> 0, of which waited for: 44 -> 0; matrix products, arithmetic and copies ran while one was open for 1% -> 0% of each run, Pallas kernels for 0% -> 0%
where the time goes in v1:
time: 69.3 us; the launch traced here: 69.1 us
  Pallas kernels  63.1 us (91%)
  local copies, waits for them, and re-layouts  5.35 us (8%)
    pallas_call x1, Pallas kernels, shards(): pl.pallas_call(functools.partial(kernel, nx, ny, nz), out_shape=(out, out...  63.1 us
    unnamed x7, local copies, waits for them, and re-layouts  5.35 us

profile of v1, /device:TPU:1, one launch (start us, length us, event | category | flops | bytes accessed | tf_op | source)
XLA Modules:
  0.0 69.1 jit_solution(8571212258401609749)
XLA Ops:
  0.6 0.0 copy-start
  0.6 1.2 %copy-done = f32[16,64,256]{2,1,0:T(8,128)S(1)} copy-done((f32[16,64,256]{2,1,0:T(8,128)S(1)}, f32[16,64,256]{2,1,0:T(8,128)}, u32[]{:S(2)}) %copy-start) | copy-done | bytes 1048600
  1.9 0.0 copy-start.1
  1.9 1.2 %copy-done.1 = f32[16,64,256]{2,1,0:T(8,128)S(1)} copy-done((f32[16,64,256]{2,1,0:T(8,128)S(1)}, f32[16,64,256]{2,1,0:T(8,128)}, u32[]{:S(2)}) %copy-start.1) | copy-done | bytes 1048600
  3.1 63.1 %shard_map.76 = (f32[16,64,256]{2,1,0:T(8,128)S(1)}, f32[16,64,256]{2,1,0:T(8,128)S(1)}, f32[16,64,256]{2,1,0:T(8,128)S(1)}) custom-call(f32[16,64,256]{2,1,0:T(8,128)S(1)} %copy-done, f32[16,64,256]{2,1,0:T(8,128)S(1)} %copy-done.1, f32[16,64,256]{2,1,0:T(8,128)} %vc_in.1, f32[16,64,256]{2,1,0:T(8,128)} %bar_in.1, s32[16,64,256]{2,1,0:T(8,128)} %act_in.1), custom_call_target="tpu_custom_call" | custom-call | tf_op jit(solution)/shard_map/pallas_call | solution.py:450
  66.2 1.0 %copy.11 = f32[16,64,256]{2,1,0:T(8,128)} copy(f32[16,64,256]{2,1,0:T(8,128)S(1)} %get-tuple-element.6) | data formatting | bytes 2097152
  67.2 1.0 %copy.12 = f32[16,64,256]{2,1,0:T(8,128)} copy(f32[16,64,256]{2,1,0:T(8,128)S(1)} %get-tuple-element.7) | data formatting | bytes 2097152
  68.2 1.0 %copy.13 = f32[16,64,256]{2,1,0:T(8,128)} copy(f32[16,64,256]{2,1,0:T(8,128)S(1)} %get-tuple-element.8) | data formatting | bytes 2097152
Async XLA Ops:
  0.6 1.2 %copy-start = (f32[16,64,256]{2,1,0:T(8,128)S(1)}, f32[16,64,256]{2,1,0:T(8,128)}, u32[]{:S(2)}) copy-start(f32[16,64,256]{2,1,0:T(8,128)} %va_in.1) | copy-start | bytes 3145732
  1.9 1.2 %copy-start.1 = (f32[16,64,256]{2,1,0:T(8,128)S(1)}, f32[16,64,256]{2,1,0:T(8,128)}, u32[]{:S(2)}) copy-start(f32[16,64,256]{2,1,0:T(8,128)} %vb_in.1) | copy-start | bytes 3145732

commit v2 on v1

v2 whole, which is shorter than its diff:
```python
import functools

import jax
import jax.numpy as jnp
from jax import lax
from jax.experimental import pallas as pl
from jax.experimental.pallas import tpu as pltpu
from jax.sharding import PartitionSpec as P

REGULAR = 0.01
CENTRE = 8.0
HALF = 7.5
STRETCH = CENTRE / HALF
Q0 = 1.0 / STRETCH
Q1 = 1.0 / (2.0 * STRETCH - Q0)
Q2 = 1.0 / (2.0 * STRETCH - Q1)
A1, B1 = Q1 * Q0, 2.0 * Q1 / HALF
A2, B2 = Q2 * Q1, 2.0 * Q2 / HALF
K1 = 1.0 + A1 + B1 * (CENTRE - 6.0)
K2 = 1.0 + A2 - 6.0 * B2
KR = B2 * CENTRE - A2
INV = 1.0 / CENTRE
INV2 = INV * INV

LANES = 128
SUB = 8
DEEP = 4
STEPS = 2
MESH = pl.DeviceIdType.MESH
WAYS = ((1, 0), (-1, 0), (0, 1), (0, -1), (1, 1), (-1, 1), (1, -1), (-1, -1))
DEEP_FIELDS = ("c1", "damp", "qc", "p1")
FLAT_FIELDS = ("v1a", "p2")
LOCAL_FIELDS = ("tmp", "u1", "uq", "kp", "rc", "e1", "e2")
OWN_FIELDS = ("open", "icd", "vb", "za", "zb", "zc")


def scratch(nx, ny, nz, mx, my):
    f32 = jnp.float32
    nt, halves = ny // SUB, nz // LANES
    shapes = {
        "raw": pltpu.VMEM((4, halves, nx, ny, LANES), f32),
        "raw_act": pltpu.VMEM((halves, nx, ny, LANES), jnp.int32),
        "ar1": pltpu.VMEM((2, my, SUB, LANES), f32),
        "ar2": pltpu.VMEM((2, mx, SUB, LANES), f32),
        "in_sem": pltpu.SemaphoreType.DMA((5, halves)),
        "out_sem": pltpu.SemaphoreType.DMA((3, 4, halves)),
        "ar_send": pltpu.SemaphoreType.DMA((2, 2)),
        "ar_recv": pltpu.SemaphoreType.DMA((2, 2)),
    }
    shapes["band"] = pltpu.VMEM((nz, nz), jnp.bfloat16)
    for name in DEEP_FIELDS + LOCAL_FIELDS:
        shapes[name] = pltpu.VMEM((nx + 2 * DEEP, nt, SUB, nz), f32)
        shapes[name + "_rim"] = pltpu.VMEM((nx + 2 * DEEP, SUB, nz), f32)
    for name in FLAT_FIELDS:
        shapes[name] = pltpu.VMEM((nx + 2, nt, SUB, nz), f32)
    for name in OWN_FIELDS:
        shapes[name] = pltpu.VMEM((nx, nt, SUB, nz), f32)
    for name in DEEP_FIELDS + FLAT_FIELDS:
        rows, pad = (DEEP, DEEP) if name in DEEP_FIELDS else (1, 0)
        for side in ("_low", "_high"):
            shapes[name + side] = pltpu.VMEM((nx + 2 * pad, rows, nz), f32)
        for side in ("_down", "_up"):
            shapes[name + side] = pltpu.VMEM((nx, rows, nz), f32)
        shapes[name + "_send"] = pltpu.SemaphoreType.DMA((8,))
        shapes[name + "_recv"] = pltpu.SemaphoreType.DMA((8,))
    return shapes


def kernel(nx, ny, nz, names, va_in, vb_in, vc_in, bar_in, act_in, out_a, out_b, out_c, *scratch_refs):
    ref = dict(zip(names, scratch_refs))
    raw, raw_act = ref["raw"], ref["raw_act"]
    gx, gy = lax.axis_index("gx"), lax.axis_index("gy")
    mx, my = lax.axis_size("gx"), lax.axis_size("gy")
    nt = ny // SUB
    halves = nz // LANES

    inputs = ((vc_in, raw.at[0]), (va_in, raw.at[1]), (act_in, raw_act), (bar_in, raw.at[2]), (vb_in, raw.at[3]))
    loads = [
        [
            pltpu.make_async_copy(src.at[:, :, pl.ds(h * LANES, LANES)], dst.at[h], ref["in_sem"].at[i, h])
            for h in range(halves)
        ]
        for i, (src, dst) in enumerate(inputs)
    ]
    for load in loads:
        for part in load:
            part.start()

    def wait_load(i):
        for part in loads[i]:
            part.wait()

    barrier = pltpu.get_barrier_semaphore()

    def greet(sx, sy):
        device = (lax.rem(gx + sx, mx), lax.rem(gy + sy, my))
        pl.semaphore_signal(barrier, inc=1, device_id=device, device_id_type=MESH)

    def greet_gy(k, carry):
        greet(0, k)
        return carry

    def greet_gx(k, carry):
        greet(k, 0)
        return carry

    lax.fori_loop(1, my, greet_gy, 0)
    lax.fori_loop(1, mx, greet_gx, 0)
    for sx in (1, mx - 1):
        for sy in (1, my - 1):
            greet(sx, sy)

    def clear(side):
        for name in DEEP_FIELDS + FLAT_FIELDS:
            edge = ref[name + side]
            edge[...] = jnp.zeros(edge.shape, jnp.float32)

    pl.when(gy == 0)(lambda: clear("_low"))
    pl.when(gy == my - 1)(lambda: clear("_high"))

    sub = lax.broadcasted_iota(jnp.int32, (SUB, LANES), 0)
    zero = jnp.zeros((SUB, LANES), jnp.float32)
    inside = jnp.where(sub < DEEP, gy, my - 1 - gy) > 0

    def span(h):
        return pl.ds(h * LANES, LANES)

    def copy_to(name, way):
        sx, sy = WAYS[way]
        deep = name in DEEP_FIELDS
        pad = DEEP if deep else 1
        if sy == 0:
            src, dst = (nx, 0) if sx > 0 else (pad, nx + pad)
            src, dst = ref[name].at[pl.ds(src, pad)], ref[name].at[pl.ds(dst, pad)]
        else:
            src, dst = ref[name + ("_up" if sy > 0 else "_down")], ref[name + ("_low" if sy > 0 else "_high")]
            if sx == 0:
                dst = dst.at[pl.ds(DEEP if deep else 0, nx)]
            else:
                src = src.at[pl.ds(nx - DEEP if sx > 0 else 0, DEEP)]
                dst = dst.at[pl.ds(0 if sx > 0 else nx + DEEP, DEEP)]
        return pltpu.make_async_remote_copy(
            src_ref=src,
            dst_ref=dst,
            send_sem=ref[name + "_send"].at[way],
            recv_sem=ref[name + "_recv"].at[way],
            device_id=(lax.rem(gx + mx + sx, mx), gy + sy),
            device_id_type=MESH,
        )

    def send_x(name):
        copy_to(name, 0).start()
        copy_to(name, 1).start()

    def along_y(name, act, taking):
        for step in (1, -1):

            @pl.when(gy < my - 1 if (step > 0) != taking else gy > 0)
            def _():
                for way, (_, sy) in enumerate(WAYS):
                    if sy == step and (name in DEEP_FIELDS or way < 4):
                        act(copy_to(name, way))

    def send_y(name):
        along_y(name, lambda copy: copy.start(), False)

    def wait_halo(name):
        copy_to(name, 0).wait_recv()
        copy_to(name, 1).wait_recv()
        along_y(name, lambda copy: copy.wait_recv(), True)

    def wait_sent(name):
        copy_to(name, 0).wait_send()
        copy_to(name, 1).wait_send()
        along_y(name, lambda copy: copy.wait_send(), False)

    def pad_of(name):
        return DEEP if name in DEEP_FIELDS + LOCAL_FIELDS else 1 if name in FLAT_FIELDS else 0

    def at(name, x, t, h):
        if t == nt:
            return ref[name + "_rim"][x + DEEP, :, span(h)]
        return ref[name][x + pad_of(name), t, :, span(h)]

    def put(name, x, t, h, value, pack=True):
        if t == nt:
            ref[name + "_rim"][x + DEEP, :, span(h)] = value
            return
        ref[name][x + pad_of(name), t, :, span(h)] = value
        if not pack:
            return
        if name in DEEP_FIELDS:
            if t < DEEP:
                ref[name + "_down"][x, t : t + 1, span(h)] = value[0:1]
            if t >= nt - DEEP:
                ref[name + "_up"][x, t - nt + DEEP : t - nt + DEEP + 1, span(h)] = value[SUB - 1 : SUB]
        elif name in FLAT_FIELDS:
            if t == 0:
                ref[name + "_down"][x, :, span(h)] = value[0:1]
            if t == nt - 1:
                ref[name + "_up"][x, :, span(h)] = value[SUB - 1 : SUB]

    def over(first, last, plane, carry=0):
        return lax.fori_loop(0, last - first, lambda k, c: plane(k + first, c), carry)

    def merge(name):
        def plane(x, carry):
            for h in range(halves):
                low, high = ref[name + "_low"][x, :, span(h)], ref[name + "_high"][x, :, span(h)]
                ref[name + "_rim"][x, :, span(h)] = jnp.concatenate([low, high], axis=0)
            return carry

        over(0, nx + 2 * DEEP, plane)

    rows = lax.broadcasted_iota(jnp.int32, (nz, nz), 0)
    columns = lax.broadcasted_iota(jnp.int32, (nz, nz), 1)
    ref["band"][...] = jnp.where(jnp.abs(rows - columns) == 1, 1.0, 0.0).astype(jnp.bfloat16)

    def along_z(values):
        top = values.astype(jnp.bfloat16)
        rest = (values - top.astype(jnp.float32)).astype(jnp.bfloat16)
        band = ref["band"][...]
        return jnp.dot(top, band, preferred_element_type=jnp.float32) + jnp.dot(
            rest, band, preferred_element_type=jnp.float32
        )

    def plane_sums(name, x, count, rim):
        flat = name in FLAT_FIELDS
        body = ref[name][pl.ds(x + pad_of(name), count)].reshape(count * ny, nz)
        z_body = along_z(body)
        if rim:
            z_rim = along_z(ref[name + "_rim"][pl.ds(x + DEEP, count)].reshape(count * SUB, nz))
        found = []
        for c in range(count):
            for t in range(nt + 1 if rim else nt):
                for h in range(halves):
                    v = at(name, x + c, t, h)
                    first, last = at(name, x + c, 0, h), at(name, x + c, nt - 1, h)
                    if t == nt:
                        before = jnp.where(sub == DEEP, pltpu.roll(last, DEEP + 1, 0), pltpu.roll(v, 1, 0))
                        after = jnp.where(sub == DEEP - 1, pltpu.roll(first, DEEP - 1, 0), pltpu.roll(v, SUB - 1, 0))
                        along = z_rim[c * SUB : (c + 1) * SUB, h * LANES : (h + 1) * LANES]
                    else:
                        if t > 0:
                            before = at(name, x + c, t - 1, h)
                        else:
                            if flat:
                                edge = ref[name + "_low"][x + c, :, span(h)]
                            else:
                                edge = pltpu.roll(at(name, x + c, nt, h), DEEP + 1, 0)
                            before = jnp.where(sub == 0, edge, pltpu.roll(last, 1, 0))
                        if t < nt - 1:
                            after = at(name, x + c, t + 1, h)
                        else:
                            if flat:
                                edge = ref[name + "_high"][x + c, :, span(h)]
                            else:
                                edge = pltpu.roll(at(name, x + c, nt, h), DEEP - 1, 0)
                            after = jnp.where(sub == SUB - 1, edge, pltpu.roll(first, SUB - 1, 0))
                        row = (c * nt + t) * SUB
                        along = z_body[row : row + SUB, h * LANES : (h + 1) * LANES]
                    sides = at(name, x + c - 1, t, h) + at(name, x + c + 1, t, h)
                    found.append((x + c, t, h, v, sides + (before + after) + along))
        return found

    def stage(f_in, f_out, make, width=0, accs=()):
        rim = width > 0
        f_outs = f_out if isinstance(f_out, tuple) else (f_out,) if f_out else ()

        def planes(first, count, accs):
            done = []
            for x, t, h, v, total in plane_sums(f_in, first, count, rim):
                value, terms = make(x, t, h, v, total)
                if t == nt:
                    value = jnp.where(inside, value, 0.0)
                else:
                    accs = tuple(a + b for a, b in zip(accs, terms))
                done.append((x, t, h, value if isinstance(value, tuple) else (value,)))
            for x, t, h, values in done:
                for name, value in zip(f_outs, values):
                    put(name, x, t, h, value)
            return accs

        if f_out in DEEP_FIELDS + FLAT_FIELDS:
            depth = DEEP
            accs = lax.fori_loop(0, 2, lambda k, a: planes(k * (nx - depth), depth, a), accs)
            send_x(f_out)
            inner = (nx - 2 * depth) // 2
            accs = lax.fori_loop(0, 2, lambda k, a: planes(depth + k * inner, inner, a), accs)
            send_y(f_out)
            return accs
        steps = STEPS
        count = (nx + 2 * width) // steps
        return lax.fori_loop(0, steps, lambda k, a: planes(k * count - width, count, a), accs)

    def first_half(x, t, h, v, total):
        return at("e1", x, t, h) * v + B1 * total, ()

    def second_half(rhs):
        def make(x, t, h, v, total):
            return at("e2", x, t, h) * v + KR * at(rhs, x, t, h) + B2 * total, ()

        return make

    def strided(buf, x, t, h):
        return buf[h, x, pl.ds(t, SUB, stride=nt), :]

    def convert(i, name):
        def plane(x, carry):
            values = [(t, h, strided(raw.at[i], x, t, h)) for t in range(nt) for h in range(halves)]
            for t, h, value in values:
                put(name, x, t, h, value)
            return carry

        over(0, nx, plane)

    wait_load(1)
    convert(1, "v1a")
    wait_load(0)
    convert(0, "c1")
    pl.semaphore_wait(barrier, mx + my + 2)
    for name in ("v1a", "c1"):
        send_x(name)
        send_y(name)
    for i in (2, 3, 4):
        wait_load(i)

    def coefficients(x, t, h, damping):
        put("e1", x, t, h, K1 - B1 * damping)
        put("e2", x, t, h, K2 - B2 * damping)

    def prepare(x, acc):
        done = []
        for t in range(nt):
            for h in range(halves):
                fixed = strided(raw_act, x, t, h).astype(jnp.float32)
                opened = 1.0 - fixed
                root = lax.rsqrt(REGULAR + strided(raw.at[2], x, t, h))
                damping = opened * root
                icd = damping * root + fixed
                vb = strided(raw.at[3], x, t, h)
                va = at("v1a", x, t, h)
                acc = acc + (va * va + vb * vb * icd)
                done.append((t, h, damping, opened, icd, vb))
        for t, h, damping, opened, icd, vb in done:
            put("damp", x, t, h, damping)
            put("open", x, t, h, opened)
            put("icd", x, t, h, icd)
            put("vb", x, t, h, vb)
            coefficients(x, t, h, damping)
        return acc

    sum_ab = over(0, nx, prepare, zero)
    send_x("damp")
    send_y("damp")

    def rim_coefficients():
        merge("damp")

        def rim(x, carry):
            for h in range(halves):
                coefficients(x, nt, h, at("damp", x, nt, h))
            return carry

        def outside(x, carry):
            for t in range(nt):
                for h in range(halves):
                    coefficients(x, t, h, at("damp", x, t, h))
            return carry

        over(-DEEP, nx + DEEP, rim)
        over(1 - DEEP, 0, outside)
        over(nx, nx + DEEP - 1, outside)

    ar1, ar2, ar_send, ar_recv = ref["ar1"], ref["ar2"], ref["ar_send"], ref["ar_recv"]

    def ar_copy(buf, i, phase, me, device):
        return pltpu.make_async_remote_copy(
            src_ref=buf.at[i, me],
            dst_ref=buf.at[i, me],
            send_sem=ar_send.at[i, phase],
            recv_sem=ar_recv.at[i, phase],
            device_id=device,
            device_id_type=MESH,
        )

    def ar_rows(i, rows):
        full = zero
        for k, row in enumerate(rows):
            full = jnp.where(sub == k, jnp.sum(row, axis=0, keepdims=True), full)
        ar1[i, gy] = full

        def go(k, carry):
            ar_copy(ar1, i, 0, gy, (gx, lax.rem(gy + k, my))).start()
            return carry

        lax.fori_loop(1, my, go, 0)

    def ar_wait(buf, i, phase, count, sem):
        whole = buf.at[i, pl.ds(0, count - 1)]
        pltpu.make_async_copy(whole, whole, sem.at[i, phase]).wait()

    def ar_middle(i):
        ar_wait(ar1, i, 0, my, ar_recv)
        full = ar1[i, 0]
        for k in range(1, my):
            full = full + ar1[i, k]
        ar2[i, gx] = full

        def go(k, carry):
            ar_copy(ar2, i, 1, gx, (lax.rem(gx + k, mx), gy)).start()
            return carry

        lax.fori_loop(1, mx, go, 0)

    def ar_end(i, count):
        ar_wait(ar2, i, 1, mx, ar_recv)
        full = ar2[i, 0]
        for k in range(1, mx):
            full = full + ar2[i, k]
        full = jnp.sum(full, axis=1, keepdims=True)
        return [jnp.broadcast_to(full[k : k + 1], (SUB, LANES)) for k in range(count)]

    def ar_sent(i):
        ar_wait(ar1, i, 0, my, ar_send)
        ar_wait(ar2, i, 1, mx, ar_send)

    def square_out(make):
        def made(x, t, h, v, total):
            value, _ = make(x, t, h, v, total)
            return value, (value * value,)

        return made

    def state_image(x, t, h, v, total):
        return 6.0 * v - total - at("open", x, t, h) * (at("vb", x, t, h) * at("icd", x, t, h)), ()

    wait_halo("v1a")
    stage("v1a", "qc", state_image)

    wait_halo("c1")
    merge("c1")
    wait_halo("damp")
    rim_coefficients()
    stage("c1", "tmp", first_half, 3)
    stage("tmp", "u1", second_half("c1"), 2)
    stage("u1", "tmp", first_half, 1)

    def last_half(x, t, h, v, total):
        value, _ = second_half("u1")(x, t, h, v, total)
        u1 = at("u1", x, t, h)
        return value, (u1 * u1, value * at("qc", x, t, h))

    sum_u, sum_qp = stage("tmp", "p1", last_half, 0, (zero, zero))
    ar_rows(0, [sum_ab + INV2 * sum_u, sum_ab + (2.0 * INV2) * sum_qp])

    wait_halo("qc")
    merge("qc")
    stage("qc", "tmp", first_half, 3)
    stage("tmp", "uq", second_half("qc"), 2)
    ar_middle(0)
    stage("uq", "tmp", first_half, 1)
    stage("tmp", "p2", second_half("uq"))

    wait_halo("p1")
    merge("p1")
    stage("p1", "kp", lambda x, t, h, v, total: (6.0 * v - total, ()), 3)
    m0, m1 = ar_end(0, 2)
    shift = m1 / m0

    def adjoint_image(x, t, h, v, total):
        damping = at("damp", x, t, h)
        part = 6.0 * v - total + damping * damping * at("p1", x, t, h)
        return INV2 * part + (1.0 - shift) * at("qc", x, t, h), ()

    stage("kp", "rc", adjoint_image, 2)
    stage("rc", "tmp", first_half, 1)
    (sum_r,) = stage("tmp", None, square_out(second_half("rc")), 0, (zero,))

    def close(x, t, h, v, total):
        va, p1 = at("v1a", x, t, h), at("p1", x, t, h)
        icd, opened, vb = at("icd", x, t, h), at("open", x, t, h), at("vb", x, t, h)
        step = INV2 * at("kp", x, t, h)
        za = (va + step) - shift * va
        ra = za + INV2 * (6.0 * v - total) - shift * step
        v2b = (1.0 - shift) * vb - opened * (INV2 * p1)
        zb = v2b * icd
        zc = INV2 * (v - shift * p1)
        rb = v2b - opened * zc
        u2 = at("uq", x, t, h) - shift * at("u1", x, t, h)
        base = za * za + zb * v2b
        return (za, zb, zc), (
            base + INV2 * (u2 * u2),
            base + 2.0 * (at("rc", x, t, h) * zc),
            ra * ra + rb * rb * icd,
        )

    wait_halo("p2")
    sums = stage("p2", ("za", "zb", "zc"), close, 0, (zero, zero, zero))
    ar_rows(1, [sums[0], sums[1], sums[2] + INV2 * sum_r])
    ar_middle(1)
    n2, top, m4 = ar_end(1, 3)

    d2 = top / n2
    g2sq = n2 / m0
    g2 = jnp.sqrt(g2sq)
    g3sq = jnp.maximum(m4 / n2 - d2 * d2 - g2sq, 0.0)
    a1 = jnp.sqrt(shift * shift + g2sq)
    c2, s2 = shift / a1, g2 / a1
    b0 = c2 * d2 - s2 * g2
    b1 = jnp.sqrt(b0 * b0 + g3sq)
    b2 = s2 * d2 + c2 * g2
    c3 = b0 / b1
    on_p = (c2 + c3 * s2 * b2 / b1) / a1
    on_z = -c3 / (b1 * a1)

    def finish(x, carry):
        done = []
        for t in range(nt):
            for h in range(halves):
                pb = at("vb", x, t, h) * at("icd", x, t, h)
                done.append((0, t, h, on_p * at("v1a", x, t, h) + on_z * at("za", x, t, h)))
                done.append((1, t, h, on_p * pb + on_z * at("zb", x, t, h)))
                done.append((2, t, h, (INV2 * on_p) * at("p1", x, t, h) + on_z * at("zc", x, t, h)))
        for i, t, h, value in done:
            raw[i, h, x, pl.ds(t, SUB, stride=nt), :] = value
        return carry

    parts = 4
    size = nx // parts
    stores = []
    for p in range(parts):
        over(p * size, (p + 1) * size, finish)
        for i, out in enumerate((out_a, out_b, out_c)):
            rows = pl.ds(p * size, size)
            for h in range(halves):
                store = pltpu.make_async_copy(
                    raw.at[i, h, rows], out.at[rows, :, pl.ds(h * LANES, LANES)], ref["out_sem"].at[i, p, h]
                )
                store.start()
                stores.append(store)
    for name in DEEP_FIELDS + FLAT_FIELDS:
        wait_sent(name)
    ar_sent(0)
    ar_sent(1)
    for store in stores:
        store.wait()


def shards(va, vb, vc, barrier, active):
    nx, ny, nz = va.shape
    hbm = pl.BlockSpec(memory_space=pltpu.HBM)
    out = jax.ShapeDtypeStruct(va.shape, jnp.float32)
    shapes = scratch(nx, ny, nz, lax.axis_size("gx"), lax.axis_size("gy"))
    return pl.pallas_call(
        functools.partial(kernel, nx, ny, nz, tuple(shapes)),
        out_shape=(out, out, out),
        in_specs=[hbm] * 5,
        out_specs=(hbm, hbm, hbm),
        scratch_shapes=list(shapes.values()),
        compiler_params=pltpu.CompilerParams(
            collective_id=0, has_side_effects=True, vmem_limit_bytes=54 * 1024 * 1024
        ),
    )(va, vb, vc, barrier, active)


def solution(mesh):
    placed = P("gx", "gy", None)
    return jax.shard_map(
        shards,
        mesh=mesh,
        in_specs=(placed,) * 5,
        out_specs=(placed,) * 3,
        check_vma=False,
    )
```

time: 69.3 us -> 63.1 us (0.911)
  Pallas kernels: 63.1 us -> 57.3 us
    pallas_call x1, Pallas kernels: 63.1 us -> 57.3 us  [shards(): pl.pallas_call(functools.partial(kernel, nx, ny, nz, tuple(shapes)), out_...]
where the time goes in v2:
time: 63.1 us; the launch traced here: 62.9 us
  Pallas kernels  57.3 us (91%)
  local copies, waits for them, and re-layouts  4.96 us (8%)
  between operations  0.65 us (1%)
    pallas_call x1, Pallas kernels, shards(): pl.pallas_call(functools.partial(kernel, nx, ny, nz, tuple(shapes)), out_...  57.3 us
    unnamed x7, local copies, waits for them, and re-layouts  4.96 us

profile of v2, /device:TPU:1, one launch (start us, length us, event | category | flops | bytes accessed | tf_op | source)
XLA Modules:
  0.0 62.9 jit_solution(14856827518046899172)
XLA Ops:
  0.6 57.3 %shard_map.76 = (f32[16,64,256]{2,1,0:T(8,128)}, f32[16,64,256]{2,1,0:T(8,128)}, f32[16,64,256]{2,1,0:T(8,128)}) custom-call(f32[16,64,256]{2,1,0:T(8,128)} %va_in.1, f32[16,64,256]{2,1,0:T(8,128)} %vb_in.1, f32[16,64,256]{2,1,0:T(8,128)} %vc_in.1, f32[16,64,256]{2,1,0:T(8,128)} %bar_in.1, s32[16,64,256]{2,1,0:T(8,128)} %act_in.1), custom_call_target="tpu_custom_call" | custom-call | tf_op jit(solution)/shard_map/pallas_call | solution.py:555
  57.9 0.0 copy-start.1
  57.9 2.4 %copy.11 = f32[16,64,256]{2,1,0:T(8,128)} copy(f32[16,64,256]{2,1,0:T(8,128)} %get-tuple-element.6) | data formatting | bytes 2097152
  60.3 0.0 copy-done.1
  60.3 0.0 copy-start
  60.3 1.0 %copy.12 = f32[16,64,256]{2,1,0:T(8,128)} copy(f32[16,64,256]{2,1,0:T(8,128)S(1)} %copy-done.1) | data formatting | bytes 2097152
  61.3 0.6 %copy-done = f32[16,64,256]{2,1,0:T(8,128)S(1)} copy-done((f32[16,64,256]{2,1,0:T(8,128)S(1)}, f32[16,64,256]{2,1,0:T(8,128)}, u32[]{:S(2)}) %copy-start) | copy-done | bytes 1048600
  61.9 1.0 %copy.13 = f32[16,64,256]{2,1,0:T(8,128)} copy(f32[16,64,256]{2,1,0:T(8,128)S(1)} %copy-done) | data formatting | bytes 2097152
Async XLA Ops:
  57.9 2.4 %copy-start.1 = (f32[16,64,256]{2,1,0:T(8,128)S(1)}, f32[16,64,256]{2,1,0:T(8,128)}, u32[]{:S(2)}) copy-start(f32[16,64,256]{2,1,0:T(8,128)} %get-tuple-element.7) | copy-start | bytes 3145732
  60.3 1.6 %copy-start = (f32[16,64,256]{2,1,0:T(8,128)S(1)}, f32[16,64,256]{2,1,0:T(8,128)}, u32[]{:S(2)}) copy-start(f32[16,64,256]{2,1,0:T(8,128)} %get-tuple-element.8) | copy-start | bytes 3145732

commit v3 on v2

--- a/solution.py
+++ b/solution.py
@@ -25,13 +25,13 @@
 LANES = 128
 SUB = 8
 DEEP = 4
-STEPS = 2
 MESH = pl.DeviceIdType.MESH
 WAYS = ((1, 0), (-1, 0), (0, 1), (0, -1), (1, 1), (-1, 1), (1, -1), (-1, -1))
 DEEP_FIELDS = ("c1", "damp", "qc", "p1")
 FLAT_FIELDS = ("v1a", "p2")
-LOCAL_FIELDS = ("tmp", "u1", "uq", "kp", "rc", "e1", "e2")
-OWN_FIELDS = ("open", "icd", "vb", "za", "zb", "zc")
+LOCAL_FIELDS = ("half", "half_q", "u1", "uq", "kp", "rc", "e1", "e2")
+OWN_FIELDS = ("open", "icd", "vb", "ur", "kp2")
+HANDED_ON = ("pa", "pb", "pc", "za", "zb", "zc")
 
 
 def scratch(nx, ny, nz, mx, my):
@@ -43,7 +43,6 @@
         "ar1": pltpu.VMEM((2, my, SUB, LANES), f32),
         "ar2": pltpu.VMEM((2, mx, SUB, LANES), f32),
         "in_sem": pltpu.SemaphoreType.DMA((5, halves)),
-        "out_sem": pltpu.SemaphoreType.DMA((3, 4, halves)),
         "ar_send": pltpu.SemaphoreType.DMA((2, 2)),
         "ar_recv": pltpu.SemaphoreType.DMA((2, 2)),
     }
@@ -66,8 +65,8 @@
     return shapes
 
 
-def kernel(nx, ny, nz, names, va_in, vb_in, vc_in, bar_in, act_in, out_a, out_b, out_c, *scratch_refs):
-    ref = dict(zip(names, scratch_refs))
+def kernel(nx, ny, nz, names, va_in, vb_in, vc_in, bar_in, act_in, *refs):
+    ref = dict(zip(HANDED_ON + ("coef",) + names, refs))
     raw, raw_act = ref["raw"], ref["raw_act"]
     gx, gy = lax.axis_index("gx"), lax.axis_index("gy")
     mx, my = lax.axis_size("gx"), lax.axis_size("gy")
@@ -96,19 +95,15 @@
         device = (lax.rem(gx + sx, mx), lax.rem(gy + sy, my))
         pl.semaphore_signal(barrier, inc=1, device_id=device, device_id_type=MESH)
 
-    def greet_gy(k, carry):
-        greet(0, k)
-        return carry
-
-    def greet_gx(k, carry):
+    far_x = sorted(range(1, mx), key=lambda k: abs(2 * k - mx))
+    far_y = sorted(range(1, my), key=lambda k: abs(2 * k - my))
+    for k in far_x:
         greet(k, 0)
-        return carry
-
-    lax.fori_loop(1, my, greet_gy, 0)
-    lax.fori_loop(1, mx, greet_gx, 0)
     for sx in (1, mx - 1):
         for sy in (1, my - 1):
             greet(sx, sy)
+    for k in far_y:
+        greet(0, k)
 
     def clear(side):
         for name in DEEP_FIELDS + FLAT_FIELDS:
@@ -130,15 +125,17 @@
         deep = name in DEEP_FIELDS
         pad = DEEP if deep else 1
         if sy == 0:
-            src, dst = (nx, 0) if sx > 0 else (pad, nx + pad)
-            src, dst = ref[name].at[pl.ds(src, pad)], ref[name].at[pl.ds(dst, pad)]
+            depth = DEEP - 1 if name == "damp" else pad
+            src, dst = (nx - depth, -depth) if sx > 0 else (0, nx)
+            src, dst = ref[name].at[pl.ds(src + pad, depth)], ref[name].at[pl.ds(dst + pad, depth)]
         else:
             src, dst = ref[name + ("_up" if sy > 0 else "_down")], ref[name + ("_low" if sy > 0 else "_high")]
             if sx == 0:
                 dst = dst.at[pl.ds(DEEP if deep else 0, nx)]
             else:
-                src = src.at[pl.ds(nx - DEEP if sx > 0 else 0, DEEP)]
-                dst = dst.at[pl.ds(0 if sx > 0 else nx + DEEP, DEEP)]
+                count = DEEP - 2 if name == "damp" else DEEP - 1
+                src = src.at[pl.ds(nx - count if sx > 0 else 0, count)]
+                dst = dst.at[pl.ds(DEEP - count if sx > 0 else nx + DEEP, count)]
         return pltpu.make_async_remote_copy(
             src_ref=src,
             dst_ref=dst,
@@ -152,27 +149,34 @@
         copy_to(name, 0).start()
         copy_to(name, 1).start()
 
-    def along_y(name, act, taking):
+    def along_y(name, act, taking, ways):
         for step in (1, -1):
 
             @pl.when(gy < my - 1 if (step > 0) != taking else gy > 0)
             def _():
-                for way, (_, sy) in enumerate(WAYS):
-                    if sy == step and (name in DEEP_FIELDS or way < 4):
+                for way in ways:
+                    if WAYS[way][1] == step:
                         act(copy_to(name, way))
 
+    def all_ways(name):
+        return range(2, 8 if name in DEEP_FIELDS else 4)
+
     def send_y(name):
-        along_y(name, lambda copy: copy.start(), False)
-
-    def wait_halo(name):
+        along_y(name, lambda copy: copy.start(), False, all_ways(name))
+
+    def wait_y(name):
+        along_y(name, lambda copy: copy.wait_recv(), True, (2, 3))
+
+    def wait_x(name):
         copy_to(name, 0).wait_recv()
         copy_to(name, 1).wait_recv()
-        along_y(name, lambda copy: copy.wait_recv(), True)
+        if name in DEEP_FIELDS:
+            along_y(name, lambda copy: copy.wait_recv(), True, (4, 5, 6, 7))
 
     def wait_sent(name):
         copy_to(name, 0).wait_send()
         copy_to(name, 1).wait_send()
-        along_y(name, lambda copy: copy.wait_send(), False)
+        along_y(name, lambda copy: copy.wait_send(), False, all_ways(name))
 
     def pad_of(name):
         return DEEP if name in DEEP_FIELDS + LOCAL_FIELDS else 1 if name in FLAT_FIELDS else 0
@@ -203,14 +207,23 @@
     def over(first, last, plane, carry=0):
         return lax.fori_loop(0, last - first, lambda k, c: plane(k + first, c), carry)
 
-    def merge(name):
+    def merge(name, first, last):
         def plane(x, carry):
             for h in range(halves):
                 low, high = ref[name + "_low"][x, :, span(h)], ref[name + "_high"][x, :, span(h)]
                 ref[name + "_rim"][x, :, span(h)] = jnp.concatenate([low, high], axis=0)
             return carry
 
-        over(0, nx + 2 * DEEP, plane)
+        over(first + DEEP, last + DEEP, plane)
+
+    def merge_inner(name):
+        wait_y(name)
+        merge(name, 0, nx)
+
+    def merge_outer(name):
+        wait_x(name)
+        merge(name, -DEEP, 0)
+        merge(name, nx, nx + DEEP)
 
     rows = lax.broadcasted_iota(jnp.int32, (nz, nz), 0)
     columns = lax.broadcasted_iota(jnp.int32, (nz, nz), 1)
@@ -224,52 +237,53 @@
             rest, band, preferred_element_type=jnp.float32
         )
 
-    def plane_sums(name, x, count, rim):
+    def plane_sums(name, parts, rim):
         flat = name in FLAT_FIELDS
-        body = ref[name][pl.ds(x + pad_of(name), count)].reshape(count * ny, nz)
-        z_body = along_z(body)
+        planes = [x + c for x, count in parts for c in range(count)]
+        body = [ref[name][pl.ds(x + pad_of(name), count)].reshape(count * ny, nz) for x, count in parts]
+        z_body = along_z(jnp.concatenate(body, axis=0))
         if rim:
-            z_rim = along_z(ref[name + "_rim"][pl.ds(x + DEEP, count)].reshape(count * SUB, nz))
+            edges = [ref[name + "_rim"][pl.ds(x + DEEP, count)].reshape(count * SUB, nz) for x, count in parts]
+            z_rim = along_z(jnp.concatenate(edges, axis=0))
         found = []
-        for c in range(count):
+        for c, x in enumerate(planes):
             for t in range(nt + 1 if rim else nt):
                 for h in range(halves):
-                    v = at(name, x + c, t, h)
-                    first, last = at(name, x + c, 0, h), at(name, x + c, nt - 1, h)
+                    v = at(name, x, t, h)
+                    first, last = at(name, x, 0, h), at(name, x, nt - 1, h)
                     if t == nt:
                         before = jnp.where(sub == DEEP, pltpu.roll(last, DEEP + 1, 0), pltpu.roll(v, 1, 0))
                         after = jnp.where(sub == DEEP - 1, pltpu.roll(first, DEEP - 1, 0), pltpu.roll(v, SUB - 1, 0))
                         along = z_rim[c * SUB : (c + 1) * SUB, h * LANES : (h + 1) * LANES]
                     else:
                         if t > 0:
-                            before = at(name, x + c, t - 1, h)
+                            before = at(name, x, t - 1, h)
                         else:
                             if flat:
-                                edge = ref[name + "_low"][x + c, :, span(h)]
+                                edge = ref[name + "_low"][x, :, span(h)]
                             else:
-                                edge = pltpu.roll(at(name, x + c, nt, h), DEEP + 1, 0)
+                                edge = pltpu.roll(at(name, x, nt, h), DEEP + 1, 0)
                             before = jnp.where(sub == 0, edge, pltpu.roll(last, 1, 0))
                         if t < nt - 1:
-                            after = at(name, x + c, t + 1, h)
+                            after = at(name, x, t + 1, h)
                         else:
                             if flat:
-                                edge = ref[name + "_high"][x + c, :, span(h)]
+                                edge = ref[name + "_high"][x, :, span(h)]
                             else:
-                                edge = pltpu.roll(at(name, x + c, nt, h), DEEP - 1, 0)
+                                edge = pltpu.roll(at(name, x, nt, h), DEEP - 1, 0)
                             after = jnp.where(sub == SUB - 1, edge, pltpu.roll(first, SUB - 1, 0))
                         row = (c * nt + t) * SUB
                         along = z_body[row : row + SUB, h * LANES : (h + 1) * LANES]
-                    sides = at(name, x + c - 1, t, h) + at(name, x + c + 1, t, h)
-                    found.append((x + c, t, h, v, sides + (before + after) + along))
+                    sides = at(name, x - 1, t, h) + at(name, x + 1, t, h)
+                    found.append((x, t, h, v, sides + (before + after) + along))
         return found
 
-    def stage(f_in, f_out, make, width=0, accs=()):
-        rim = width > 0
+    def stage(f_in, f_out, make, parts, accs=(), rim=True, steps=1):
         f_outs = f_out if isinstance(f_out, tuple) else (f_out,) if f_out else ()
 
-        def planes(first, count, accs):
+        def some(parts, accs):
             done = []
-            for x, t, h, v, total in plane_sums(f_in, first, count, rim):
+            for x, t, h, v, total in plane_sums(f_in, parts, rim):
                 value, terms = make(x, t, h, v, total)
                 if t == nt:
                     value = jnp.where(inside, value, 0.0)
@@ -281,17 +295,19 @@
                     put(name, x, t, h, value)
             return accs
 
-        if f_out in DEEP_FIELDS + FLAT_FIELDS:
-            depth = DEEP
-            accs = lax.fori_loop(0, 2, lambda k, a: planes(k * (nx - depth), depth, a), accs)
-            send_x(f_out)
-            inner = (nx - 2 * depth) // 2
-            accs = lax.fori_loop(0, 2, lambda k, a: planes(depth + k * inner, inner, a), accs)
-            send_y(f_out)
-            return accs
-        steps = STEPS
-        count = (nx + 2 * width) // steps
-        return lax.fori_loop(0, steps, lambda k, a: planes(k * count - width, count, a), accs)
+        if steps == 1:
+            return some(parts, accs)
+        ((first, count),) = parts
+        size = count // steps
+        return lax.fori_loop(0, steps, lambda k, a: some([(first + k * size, size)], a), accs)
+
+    def inner(f_in, f_out, make, width, accs=()):
+        count = nx - 2 * (DEEP - width)
+        steps = next(k for k in (4, 3, 2, 1) if count % k == 0 and count // k > 3)
+        return stage(f_in, f_out, make, [(DEEP - width, count)], accs, width > 0, steps)
+
+    def outer(f_in, f_out, make, width, accs=()):
+        return stage(f_in, f_out, make, [(-width, DEEP), (nx + width - DEEP, DEEP)], accs, width > 0)
 
     def first_half(x, t, h, v, total):
         return at("e1", x, t, h) * v + B1 * total, ()
@@ -354,23 +370,23 @@
     send_x("damp")
     send_y("damp")
 
-    def rim_coefficients():
-        merge("damp")
-
+    def rim_coefficients(first, last):
         def rim(x, carry):
             for h in range(halves):
                 coefficients(x, nt, h, at("damp", x, nt, h))
             return carry
 
+        over(first, last, rim)
+
+    def outer_coefficients(first, last):
         def outside(x, carry):
-            for t in range(nt):
-                for h in range(halves):
-                    coefficients(x, t, h, at("damp", x, t, h))
+            values = [(t, h, at("damp", x, t, h)) for t in range(nt) for h in range(halves)]
+            for t, h, value in values:
+                coefficients(x, t, h, value)
             return carry
 
-        over(-DEEP, nx + DEEP, rim)
-        over(1 - DEEP, 0, outside)
-        over(nx, nx + DEEP - 1, outside)
+        rim_coefficients(first, last)
+        over(first, last, outside)
 
     ar1, ar2, ar_send, ar_recv = ref["ar1"], ref["ar2"], ref["ar_send"], ref["ar_recv"]
 
@@ -390,11 +406,8 @@
             full = jnp.where(sub == k, jnp.sum(row, axis=0, keepdims=True), full)
         ar1[i, gy] = full
 
-        def go(k, carry):
+        for k in far_y:
             ar_copy(ar1, i, 0, gy, (gx, lax.rem(gy + k, my))).start()
-            return carry
-
-        lax.fori_loop(1, my, go, 0)
 
     def ar_wait(buf, i, phase, count, sem):
         whole = buf.at[i, pl.ds(0, count - 1)]
@@ -407,11 +420,8 @@
             full = full + ar1[i, k]
         ar2[i, gx] = full
 
-        def go(k, carry):
+        for k in far_x:
             ar_copy(ar2, i, 1, gx, (lax.rem(gx + k, mx), gy)).start()
-            return carry
-
-        lax.fori_loop(1, mx, go, 0)
 
     def ar_end(i, count):
         ar_wait(ar2, i, 1, mx, ar_recv)
@@ -435,69 +445,111 @@
     def state_image(x, t, h, v, total):
         return 6.0 * v - total - at("open", x, t, h) * (at("vb", x, t, h) * at("icd", x, t, h)), ()
 
-    wait_halo("v1a")
-    stage("v1a", "qc", state_image)
-
-    wait_halo("c1")
-    merge("c1")
-    wait_halo("damp")
-    rim_coefficients()
-    stage("c1", "tmp", first_half, 3)
-    stage("tmp", "u1", second_half("c1"), 2)
-    stage("u1", "tmp", first_half, 1)
+    wait_y("v1a")
+    wait_x("v1a")
+    stage("v1a", "qc", state_image, [(0, DEEP), (nx - DEEP, DEEP)], rim=False)
+    send_x("qc")
+    stage("v1a", "qc", state_image, [(DEEP, nx - 2 * DEEP)], rim=False, steps=2)
+    send_y("qc")
 
     def last_half(x, t, h, v, total):
         value, _ = second_half("u1")(x, t, h, v, total)
         u1 = at("u1", x, t, h)
         return value, (u1 * u1, value * at("qc", x, t, h))
 
-    sum_u, sum_qp = stage("tmp", "p1", last_half, 0, (zero, zero))
+    def first_chain(part, accs):
+        part("c1", "half", first_half, 3)
+        part("half", "u1", second_half("c1"), 2)
+        part("u1", "half", first_half, 1)
+        return part("half", "p1", last_half, 0, accs)
+
+    def second_chain(part):
+        part("qc", "half_q", first_half, 3)
+        part("half_q", "uq", second_half("qc"), 2)
+        part("uq", "half_q", first_half, 1)
+        part("half_q", "p2", second_half("uq"), 0)
+
+    merge_inner("c1")
+    merge_inner("damp")
+    rim_coefficients(0, nx)
+    accs = first_chain(inner, (zero, zero))
+    merge_inner("qc")
+    second_chain(inner)
+
+    merge_outer("c1")
+    merge_outer("damp")
+    outer_coefficients(1 - DEEP, 0)
+    outer_coefficients(nx, nx + DEEP - 1)
+    sum_u, sum_qp = first_chain(outer, accs)
+    send_x("p1")
+    send_y("p1")
     ar_rows(0, [sum_ab + INV2 * sum_u, sum_ab + (2.0 * INV2) * sum_qp])
 
-    wait_halo("qc")
-    merge("qc")
-    stage("qc", "tmp", first_half, 3)
-    stage("tmp", "uq", second_half("qc"), 2)
+    merge_outer("qc")
     ar_middle(0)
-    stage("uq", "tmp", first_half, 1)
-    stage("tmp", "p2", second_half("uq"))
-
-    wait_halo("p1")
-    merge("p1")
-    stage("p1", "kp", lambda x, t, h, v, total: (6.0 * v - total, ()), 3)
-    m0, m1 = ar_end(0, 2)
-    shift = m1 / m0
+    second_chain(outer)
+    send_x("p2")
+    send_y("p2")
 
     def adjoint_image(x, t, h, v, total):
         damping = at("damp", x, t, h)
         part = 6.0 * v - total + damping * damping * at("p1", x, t, h)
-        return INV2 * part + (1.0 - shift) * at("qc", x, t, h), ()
-
-    stage("kp", "rc", adjoint_image, 2)
-    stage("rc", "tmp", first_half, 1)
-    (sum_r,) = stage("tmp", None, square_out(second_half("rc")), 0, (zero,))
-
-    def close(x, t, h, v, total):
-        va, p1 = at("v1a", x, t, h), at("p1", x, t, h)
-        icd, opened, vb = at("icd", x, t, h), at("open", x, t, h), at("vb", x, t, h)
-        step = INV2 * at("kp", x, t, h)
-        za = (va + step) - shift * va
-        ra = za + INV2 * (6.0 * v - total) - shift * step
-        v2b = (1.0 - shift) * vb - opened * (INV2 * p1)
-        zb = v2b * icd
-        zc = INV2 * (v - shift * p1)
-        rb = v2b - opened * zc
-        u2 = at("uq", x, t, h) - shift * at("u1", x, t, h)
-        base = za * za + zb * v2b
-        return (za, zb, zc), (
-            base + INV2 * (u2 * u2),
-            base + 2.0 * (at("rc", x, t, h) * zc),
-            ra * ra + rb * rb * icd,
-        )
-
-    wait_halo("p2")
-    sums = stage("p2", ("za", "zb", "zc"), close, 0, (zero, zero, zero))
-    ar_rows(1, [sums[0], sums[1], sums[2] + INV2 * sum_r])
+        return INV2 * part + at("qc", x, t, h), ()
+
+    def image(x, t, h, v, total):
+        return 6.0 * v - total, ()
+
+    def third_chain(part):
+        part("p1", "kp", image, 3)
+        part("kp", "rc", adjoint_image, 2)
+        part("rc", "half", first_half, 1)
+        part("half", "ur", second_half("rc"), 0)
+
+    merge_inner("p1")
+    third_chain(inner)
+    wait_y("p2")
+    stage("p2", "kp2", image, [(1, nx - 2)], rim=False, steps=2)
+    merge_outer("p1")
+    third_chain(outer)
+    wait_x("p2")
+    stage("p2", "kp2", image, [(0, 1), (nx - 1, 1)], rim=False)
+    m0, m1 = ar_end(0, 2)
+    shift = m1 / m0
+
+    def close(x, accs):
+        done = []
+        for t in range(nt):
+            for h in range(halves):
+                va, p1 = at("v1a", x, t, h), INV2 * at("p1", x, t, h)
+                icd, opened, vb = at("icd", x, t, h), at("open", x, t, h), at("vb", x, t, h)
+                step, uq = INV2 * at("kp", x, t, h), at("uq", x, t, h)
+                za = (va + step) - shift * va
+                ra = za + INV2 * at("kp2", x, t, h) - shift * step
+                v2b = (1.0 - shift) * vb - opened * p1
+                zb = v2b * icd
+                zc = INV2 * at("p2", x, t, h) - shift * p1
+                rb = v2b - opened * zc
+                rc = at("rc", x, t, h) - shift * at("qc", x, t, h)
+                u2 = uq - shift * at("u1", x, t, h)
+                ur = at("ur", x, t, h) - shift * uq
+                base = za * za + zb * v2b
+                terms = (
+                    base + INV2 * (u2 * u2),
+                    base + 2.0 * (rc * zc),
+                    ra * ra + rb * rb * icd + INV2 * (ur * ur),
+                )
+                accs = tuple(a + b for a, b in zip(accs, terms))
+                done.append((t, h, (va, vb * icd, p1, za, zb, zc)))
+        for t, h, values in done:
+            for name, value in zip(HANDED_ON, values):
+                put(name, x, t, h, value)
+        return accs
+
+    sums = over(0, nx, close, (zero, zero, zero))
+    ar_rows(1, sums)
+    for name in DEEP_FIELDS + FLAT_FIELDS:
+        wait_sent(name)
+    ar_sent(0)
     ar_middle(1)
     n2, top, m4 = ar_end(1, 3)
 
@@ -511,57 +563,70 @@
     b1 = jnp.sqrt(b0 * b0 + g3sq)
     b2 = s2 * d2 + c2 * g2
     c3 = b0 / b1
-    on_p = (c2 + c3 * s2 * b2 / b1) / a1
-    on_z = -c3 / (b1 * a1)
+    ref["coef"][0] = (c2 + c3 * s2 * b2 / b1) / a1
+    ref["coef"][1] = -c3 / (b1 * a1)
+    ar_sent(1)
+
+
+def combine(nx, ny, nz, pa, pb, pc, za, zb, zc, coef, out_a, out_b, out_c, raw, out_sem):
+    nt, halves, parts = ny // SUB, nz // LANES, 4
+    on_p, on_z = coef[0], coef[1]
+    outs = ((pa, za, out_a), (pb, zb, out_b), (pc, zc, out_c))
 
     def finish(x, carry):
         done = []
-        for t in range(nt):
-            for h in range(halves):
-                pb = at("vb", x, t, h) * at("icd", x, t, h)
-                done.append((0, t, h, on_p * at("v1a", x, t, h) + on_z * at("za", x, t, h)))
-                done.append((1, t, h, on_p * pb + on_z * at("zb", x, t, h)))
-                done.append((2, t, h, (INV2 * on_p) * at("p1", x, t, h) + on_z * at("zc", x, t, h)))
+        for i, (p, z, _) in enumerate(outs):
+            for t in range(nt):
+                for h in range(halves):
+                    span = pl.ds(h * LANES, LANES)
+                    done.append((i, t, h, on_p * p[x, t, :, span] + on_z * z[x, t, :, span]))
         for i, t, h, value in done:
             raw[i, h, x, pl.ds(t, SUB, stride=nt), :] = value
         return carry
 
-    parts = 4
     size = nx // parts
     stores = []
-    for p in range(parts):
-        over(p * size, (p + 1) * size, finish)
-        for i, out in enumerate((out_a, out_b, out_c)):
-            rows = pl.ds(p * size, size)
+    for part in range(parts):
+        lax.fori_loop(part * size, (part + 1) * size, finish, 0)
+        for i, (_, _, out) in enumerate(outs):
+            rows = pl.ds(part * size, size)
             for h in range(halves):
-                store = pltpu.make_async_copy(
-                    raw.at[i, h, rows], out.at[rows, :, pl.ds(h * LANES, LANES)], ref["out_sem"].at[i, p, h]
-                )
+                to = out.at[rows, :, pl.ds(h * LANES, LANES)]
+                store = pltpu.make_async_copy(raw.at[i, h, rows], to, out_sem.at[i, part, h])
                 store.start()
                 stores.append(store)
-    for name in DEEP_FIELDS + FLAT_FIELDS:
-        wait_sent(name)
-    ar_sent(0)
-    ar_sent(1)
     for store in stores:
         store.wait()
 
 
 def shards(va, vb, vc, barrier, active):
     nx, ny, nz = va.shape
+    nt, halves = ny // SUB, nz // LANES
+    f32 = jnp.float32
     hbm = pl.BlockSpec(memory_space=pltpu.HBM)
-    out = jax.ShapeDtypeStruct(va.shape, jnp.float32)
+    vmem = pl.BlockSpec(memory_space=pltpu.VMEM)
     shapes = scratch(nx, ny, nz, lax.axis_size("gx"), lax.axis_size("gy"))
-    return pl.pallas_call(
+    handed = (jax.ShapeDtypeStruct((nx, nt, SUB, nz), f32),) * len(HANDED_ON)
+    handed += (jax.ShapeDtypeStruct((2, SUB, LANES), f32),)
+    found = pl.pallas_call(
         functools.partial(kernel, nx, ny, nz, tuple(shapes)),
-        out_shape=(out, out, out),
+        out_shape=handed,
         in_specs=[hbm] * 5,
-        out_specs=(hbm, hbm, hbm),
+        out_specs=(vmem,) * len(handed),
         scratch_shapes=list(shapes.values()),
         compiler_params=pltpu.CompilerParams(
-            collective_id=0, has_side_effects=True, vmem_limit_bytes=54 * 1024 * 1024
+            collective_id=0, has_side_effects=True, vmem_limit_bytes=47 * 1024 * 1024
         ),
     )(va, vb, vc, barrier, active)
+    out = jax.ShapeDtypeStruct(va.shape, f32)
+    return pl.pallas_call(
+        functools.partial(combine, nx, ny, nz),
+        out_shape=(out,) * 3,
+        in_specs=[vmem] * len(handed),
+        out_specs=(hbm,) * 3,
+        scratch_shapes=[pltpu.VMEM((3, halves, nx, ny, LANES), f32), pltpu.SemaphoreType.DMA((3, 4, halves))],
+        compiler_params=pltpu.CompilerParams(vmem_limit_bytes=6 * 1024 * 1024),
+    )(*found)
 
 
 def solution(mesh):

time: 63.1 us -> 53.3 us (0.84)
  local copies, waits for them, and re-layouts: 4.96 us -> 0 us
  Pallas kernels: 57.3 us -> 52.6 us
    pallas_call x1, Pallas kernels: 57.3 us -> 50.5 us  [shards(): pl.pallas_call(functools.partial(kernel, nx, ny, nz, tuple(shapes)), out_...]
    unnamed x7 -> x0, local copies, waits for them, and re-layouts: 4.96 us -> none
    pallas_call x0 -> x1, Pallas kernels: none -> 2.01 us  [shards(): pl.pallas_call(functools.partial(combine, nx, ny, nz), out_shape=(out,) *...]
where the time goes in v3:
time: 53.3 us; the launch traced here: 53.2 us
  Pallas kernels  52.6 us (99%)
  between operations  0.64 us (1%)
    pallas_call x1, Pallas kernels, shards(): pl.pallas_call(functools.partial(kernel, nx, ny, nz, tuple(shapes)), out_...  50.5 us
    pallas_call x1, Pallas kernels, shards(): pl.pallas_call(functools.partial(combine, nx, ny, nz), out_shape=(out,) *...  2.01 us

profile of v3, /device:TPU:1, one launch (start us, length us, event | category | flops | bytes accessed | tf_op | source)
XLA Modules:
  0.0 53.2 jit_solution(12340798851199546782)
XLA Ops:
  0.6 50.5 %shard_map.76 = (f32[16,8,8,256]{3,2,1,0:T(8,128)S(1)}, f32[16,8,8,256]{3,2,1,0:T(8,128)S(1)}, f32[16,8,8,256]{3,2,1,0:T(8,128)S(1)}, f32[16,8,8,256]{3,2,1,0:T(...) custom-call(f32[16,64,256]{2,1,0:T(8,128)} %va_in.1, ...), custom_call_target="tpu_custom_call" | custom-call | tf_op jit(solution)/shard_map/pallas_call | solution.py:611
  51.2 2.0 %shard_map.77 = (f32[16,64,256]{2,1,0:T(8,128)}, f32[16,64,256]{2,1,0:T(8,128)}, f32[16,64,256]{2,1,0:T(8,128)}) custom-call(f32[16,8,8,256]{3,2,1,0:T(8,128)S(1)} %get-tuple-element.10.pa, f32[16,8,8,256]{3,2,1,0:T(8,128)S(1)} %get-tuple-element.11.pb, f32[16,8,8,256]{3,2,1,0:T(8,128)S(1)} %get-tuple-element.12.pc, ...), custom_call_target="tpu_custom_call" | custom-call | tf_op jit(solution)/shard_map/pallas_call | solution.py:622

commit v4 on v3

--- a/solution.py
+++ b/solution.py
@@ -43,6 +43,10 @@
         "ar1": pltpu.VMEM((2, my, SUB, LANES), f32),
         "ar2": pltpu.VMEM((2, mx, SUB, LANES), f32),
         "in_sem": pltpu.SemaphoreType.DMA((5, halves)),
+        "half_send": pltpu.SemaphoreType.DMA((2,)),
+        "half_recv": pltpu.SemaphoreType.DMA((2,)),
+        "half_q_send": pltpu.SemaphoreType.DMA((2,)),
+        "half_q_recv": pltpu.SemaphoreType.DMA((2,)),
         "ar_send": pltpu.SemaphoreType.DMA((2, 2)),
         "ar_recv": pltpu.SemaphoreType.DMA((2, 2)),
     }
@@ -125,7 +129,7 @@
         deep = name in DEEP_FIELDS
         pad = DEEP if deep else 1
         if sy == 0:
-            depth = DEEP - 1 if name == "damp" else pad
+            depth = {"c1": DEEP - 1, "qc": DEEP - 1, "damp": DEEP - 2}.get(name, pad)
             src, dst = (nx - depth, -depth) if sx > 0 else (0, nx)
             src, dst = ref[name].at[pl.ds(src + pad, depth)], ref[name].at[pl.ds(dst + pad, depth)]
         else:
@@ -177,6 +181,17 @@
         copy_to(name, 0).wait_send()
         copy_to(name, 1).wait_send()
         along_y(name, lambda copy: copy.wait_send(), False, all_ways(name))
+
+    def half_copy(name, way):
+        src, dst = (nx - DEEP + 1, 1 - DEEP) if way == 0 else (DEEP - 2, nx + DEEP - 2)
+        return pltpu.make_async_remote_copy(
+            src_ref=ref[name].at[src + DEEP],
+            dst_ref=ref[name].at[dst + DEEP],
+            send_sem=ref[name + "_send"].at[way],
+            recv_sem=ref[name + "_recv"].at[way],
+            device_id=(lax.rem(gx + mx + WAYS[way][0], mx), gy),
+            device_id_type=MESH,
+        )
 
     def pad_of(name):
         return DEEP if name in DEEP_FIELDS + LOCAL_FIELDS else 1 if name in FLAT_FIELDS else 0
@@ -334,10 +349,6 @@
     convert(1, "v1a")
     wait_load(0)
     convert(0, "c1")
-    pl.semaphore_wait(barrier, mx + my + 2)
-    for name in ("v1a", "c1"):
-        send_x(name)
-        send_y(name)
     for i in (2, 3, 4):
         wait_load(i)
 
@@ -367,8 +378,10 @@
         return acc
 
     sum_ab = over(0, nx, prepare, zero)
-    send_x("damp")
-    send_y("damp")
+    pl.semaphore_wait(barrier, mx + my + 2)
+    for name in ("v1a", "c1", "damp"):
+        send_x(name)
+        send_y(name)
 
     def rim_coefficients(first, last):
         def rim(x, carry):
@@ -445,6 +458,42 @@
     def state_image(x, t, h, v, total):
         return 6.0 * v - total - at("open", x, t, h) * (at("vb", x, t, h) * at("icd", x, t, h)), ()
 
+    def last_half(x, t, h, v, total):
+        value, _ = second_half("u1")(x, t, h, v, total)
+        u1 = at("u1", x, t, h)
+        return value, (u1 * u1, value * at("qc", x, t, h))
+
+    def first_chain(part, accs):
+        part("half", "u1", second_half("c1"), 2)
+        part("u1", "half", first_half, 1)
+        return part("half", "p1", last_half, 0, accs)
+
+    def second_chain(part):
+        part("half_q", "uq", second_half("qc"), 2)
+
+    def second_chain_end(part):
+        part("uq", "half_q", first_half, 1)
+        part("half_q", "p2", second_half("uq"), 0)
+
+    merge_inner("c1")
+    merge_inner("damp")
+    rim_coefficients(0, nx)
+    def start_inner(rhs, half):
+        stage(rhs, half, first_half, [(DEEP - 2, 1), (nx - DEEP + 1, 1)])
+        half_copy(half, 0).start()
+        half_copy(half, 1).start()
+
+    def rest_inner(rhs, half):
+        stage(rhs, half, first_half, [(1, 1), (nx - 2, 1)])
+        stage(rhs, half, first_half, [(DEEP - 1, nx - 2 * DEEP + 2)], steps=2)
+
+    def start_outer(rhs, half):
+        stage(rhs, half, first_half, [(2 - DEEP, DEEP - 1), (nx - 1, DEEP - 1)])
+        half_copy(half, 0).wait()
+        half_copy(half, 1).wait()
+
+    start_inner("c1", "half")
+
     wait_y("v1a")
     wait_x("v1a")
     stage("v1a", "qc", state_image, [(0, DEEP), (nx - DEEP, DEEP)], rim=False)
@@ -452,44 +501,31 @@
     stage("v1a", "qc", state_image, [(DEEP, nx - 2 * DEEP)], rim=False, steps=2)
     send_y("qc")
 
-    def last_half(x, t, h, v, total):
-        value, _ = second_half("u1")(x, t, h, v, total)
-        u1 = at("u1", x, t, h)
-        return value, (u1 * u1, value * at("qc", x, t, h))
-
-    def first_chain(part, accs):
-        part("c1", "half", first_half, 3)
-        part("half", "u1", second_half("c1"), 2)
-        part("u1", "half", first_half, 1)
-        return part("half", "p1", last_half, 0, accs)
-
-    def second_chain(part):
-        part("qc", "half_q", first_half, 3)
-        part("half_q", "uq", second_half("qc"), 2)
-        part("uq", "half_q", first_half, 1)
-        part("half_q", "p2", second_half("uq"), 0)
-
-    merge_inner("c1")
-    merge_inner("damp")
-    rim_coefficients(0, nx)
+    rest_inner("c1", "half")
     accs = first_chain(inner, (zero, zero))
     merge_inner("qc")
+    start_inner("qc", "half_q")
+    rest_inner("qc", "half_q")
     second_chain(inner)
 
     merge_outer("c1")
     merge_outer("damp")
-    outer_coefficients(1 - DEEP, 0)
-    outer_coefficients(nx, nx + DEEP - 1)
+    outer_coefficients(2 - DEEP, 0)
+    outer_coefficients(nx, nx + DEEP - 2)
+    start_outer("c1", "half")
     sum_u, sum_qp = first_chain(outer, accs)
     send_x("p1")
     send_y("p1")
     ar_rows(0, [sum_ab + INV2 * sum_u, sum_ab + (2.0 * INV2) * sum_qp])
 
+    second_chain_end(inner)
     merge_outer("qc")
-    ar_middle(0)
+    start_outer("qc", "half_q")
     second_chain(outer)
+    second_chain_end(outer)
     send_x("p2")
     send_y("p2")
+    ar_middle(0)
 
     def adjoint_image(x, t, h, v, total):
         damping = at("damp", x, t, h)

time: 53.3 us -> 51.9 us (0.974)
  Pallas kernels: 52.6 us -> 51.1 us
    pallas_call x1, Pallas kernels: 50.5 us -> 49.1 us  [shards(): pl.pallas_call(functools.partial(kernel, nx, ny, nz, tuple(shapes)), out_...]
where the time goes in v4:
time: 51.9 us; the launch traced here: 51.8 us
  Pallas kernels  51.1 us (98%)
  between operations  0.64 us (1%)
    pallas_call x1, Pallas kernels, shards(): pl.pallas_call(functools.partial(kernel, nx, ny, nz, tuple(shapes)), out_...  49.1 us
    pallas_call x1, Pallas kernels, shards(): pl.pallas_call(functools.partial(combine, nx, ny, nz), out_shape=(out,) *...  2.01 us

profile of v4, /device:TPU:1, one launch (start us, length us, event | category | flops | bytes accessed | tf_op | source)
XLA Modules:
  0.0 51.8 jit_solution(3622181203640456547)
XLA Ops:
  0.6 49.1 %shard_map.76 = (f32[16,8,8,256]{3,2,1,0:T(8,128)S(1)}, f32[16,8,8,256]{3,2,1,0:T(8,128)S(1)}, f32[16,8,8,256]{3,2,1,0:T(8,128)S(1)}, f32[16,8,8,256]{3,2,1,0:T(...) custom-call(f32[16,64,256]{2,1,0:T(8,128)} %va_in.1, ...), custom_call_target="tpu_custom_call" | custom-call | tf_op jit(solution)/shard_map/pallas_call | solution.py:647
  49.7 2.0 %shard_map.77 = (f32[16,64,256]{2,1,0:T(8,128)}, f32[16,64,256]{2,1,0:T(8,128)}, f32[16,64,256]{2,1,0:T(8,128)}) custom-call(f32[16,8,8,256]{3,2,1,0:T(8,128)S(1)} %get-tuple-element.10.pa, f32[16,8,8,256]{3,2,1,0:T(8,128)S(1)} %get-tuple-element.11.pb, f32[16,8,8,256]{3,2,1,0:T(8,128)S(1)} %get-tuple-element.12.pc, ...), custom_call_target="tpu_custom_call" | custom-call | tf_op jit(solution)/shard_map/pallas_call | solution.py:658
